TPU v7x, 32 devices: a whole 2x2x4 slice. The times are simulated.
32 devices in a mesh: row: 2 (over x), col: 16 (over z, y, core).
Axes of the slice: x: 2, y: 2, z: 4, core: 2. Of those that a mesh axis runs over, the one named last changes fastest.
Arguments:
- tokens: bfloat16 [160, 8192], P('col', 'row'), may hold values from -6 to 6
- cotangent: bfloat16 [160, 8192], P('col', 'row'), may hold values from -6 to 6
- gate_tiles: bfloat16 [12, 2048, 128], P('row', 'col'), may hold values from -0.125 to 0.125
- up_tiles: bfloat16 [12, 2048, 128], P('row', 'col'), may hold values from -0.125 to 0.125
- down_tiles: bfloat16 [12, 2048, 128], P('row', 'col'), may hold values from -0.09375 to 0.09375
- tile_index: int32 [3, 12, 32], P(None, 'row', 'col'), may hold values from 0 to 31, as said below
- tile_counts: int32 [3, 2, 16], P(None, 'row', 'col'), may hold values from 1 to 6, as said below
Outputs:
- output: bfloat16 [160, 8192], P('col', 'row')
- input_grad: bfloat16 [160, 8192], P('col', 'row')
- gate_grad: float32 [12, 2048, 128], P('row', 'col')
- up_grad: float32 [12, 2048, 128], P('row', 'col')
- down_grad: float32 [12, 2048, 128], P('row', 'col')
Inputs may be any that keep to these rules, and one draw needn't show every extreme that they name: `tile_index`: within one matrix, row group and column group, the 6 slots name distinct block pairs; for gate and up the row block is below 32 and the column block below 8, for down the row block is below 8 and the column block below 32. `tile_counts`: for each matrix some row group and column group has all 6 slots live.
All inputs are finite; a program needn't handle non-finite values.
Results may differ from a plain program's by a relative error of at most 0.0049.
Values may be sent and summed in bfloat16 or wider, within the bound.
A program may use at most 64 MiB of HBM per device.

v0:
```python
import jax
import jax.numpy as jnp
from jax import lax
from jax.sharding import PartitionSpec as P

FF = 16384


def pick_blocks(data_rows, block_ids, tile_size):
    token_count = data_rows.shape[0]
    block_count = data_rows.shape[1] // tile_size
    split_rows = data_rows.reshape(token_count, block_count, tile_size)
    select = (block_ids[:, None] == jnp.arange(block_count)[None, :]).astype(jnp.bfloat16)
    picked = jnp.einsum("tbk,sb->tsk", split_rows, select, preferred_element_type=jnp.float32)
    return picked.astype(jnp.bfloat16)


def place_blocks(products, block_ids, live_mask, block_count):
    select = ((block_ids[:, None] == jnp.arange(block_count)[None, :]) & live_mask[:, None]).astype(
        jnp.float32
    )
    placed = jnp.einsum("tsn,sc->tcn", products, select, precision=lax.Precision.HIGHEST)
    return placed.reshape(products.shape[0], block_count * products.shape[2])


def sparse_apply(data_rows, tiles, in_ids, out_ids, live_mask, out_count):
    picked = pick_blocks(data_rows, in_ids, tiles.shape[-1])
    products = jnp.einsum("tsk,skn->tsn", picked, tiles, preferred_element_type=jnp.float32)
    return place_blocks(products, out_ids, live_mask, out_count)


def sparse_apply_back(data_rows, tiles, in_ids, out_ids, live_mask, out_count):
    picked = pick_blocks(data_rows, in_ids, tiles.shape[-1])
    products = jnp.einsum("tsn,skn->tsk", picked, tiles, preferred_element_type=jnp.float32)
    return place_blocks(products, out_ids, live_mask, out_count)


def tile_grads(left_rows, right_rows, left_ids, right_ids, live_mask, tile_size):
    left_picked = pick_blocks(left_rows, left_ids, tile_size)
    right_picked = pick_blocks(right_rows, right_ids, tile_size)
    gradient = jnp.einsum(
        "tsk,tsn->skn", left_picked, right_picked, preferred_element_type=jnp.float32
    )
    return jnp.where(live_mask[:, None, None], gradient, jnp.zeros_like(gradient))


def gated_units(gate_sum, up_sum, hidden_grad):
    sigmoid_gate = jax.nn.sigmoid(gate_sum)
    active = gate_sum * sigmoid_gate
    hidden = (active * up_sum).astype(jnp.bfloat16)
    gate_act = (
        hidden_grad * up_sum * sigmoid_gate * (1.0 + gate_sum * (1.0 - sigmoid_gate))
    ).astype(jnp.bfloat16)
    up_act = (hidden_grad * active).astype(jnp.bfloat16)
    return (hidden, gate_act, up_act)


def body(tokens, cotangent, gate_tiles, up_tiles, down_tiles, tile_index, tile_counts):
    tile_size = gate_tiles.shape[-1]
    row_blocks = tokens.shape[1] // tile_size
    col_blocks = FF // lax.axis_size("col") // tile_size
    slot_ids = jnp.arange(gate_tiles.shape[0])
    gate_live = slot_ids < tile_counts[0, 0, 0]
    up_live = slot_ids < tile_counts[1, 0, 0]
    down_live = slot_ids < tile_counts[2, 0, 0]
    gate_in, gate_out = (tile_index[0, :, 0], tile_index[0, :, 1])
    up_in, up_out = (tile_index[1, :, 0], tile_index[1, :, 1])
    down_in, down_out = (tile_index[2, :, 0], tile_index[2, :, 1])
    whole_tokens, whole_cotangent = (
        lax.all_gather(tokens, "col", axis=0, tiled=True),
        lax.all_gather(cotangent, "col", axis=0, tiled=True),
    )
    gate_part = sparse_apply(whole_tokens, gate_tiles, gate_in, gate_out, gate_live, col_blocks)
    up_part = sparse_apply(whole_tokens, up_tiles, up_in, up_out, up_live, col_blocks)
    grad_part = sparse_apply_back(
        whole_cotangent, down_tiles, down_out, down_in, down_live, col_blocks
    )
    gate_sum, up_sum, hidden_grad = (
        lax.psum_scatter(gate_part, "row", scatter_dimension=0, tiled=True),
        lax.psum_scatter(up_part, "row", scatter_dimension=0, tiled=True),
        lax.psum_scatter(grad_part, "row", scatter_dimension=0, tiled=True),
    )
    hidden, gate_act, up_act = gated_units(gate_sum, up_sum, hidden_grad)
    hidden_all, gate_all, up_all = (
        lax.all_gather(hidden, "row", axis=0, tiled=True),
        lax.all_gather(gate_act, "row", axis=0, tiled=True),
        lax.all_gather(up_act, "row", axis=0, tiled=True),
    )
    output_part = sparse_apply(hidden_all, down_tiles, down_in, down_out, down_live, row_blocks)
    input_part = sparse_apply_back(gate_all, gate_tiles, gate_out, gate_in, gate_live, row_blocks)
    input_part = input_part + sparse_apply_back(
        up_all, up_tiles, up_out, up_in, up_live, row_blocks
    )
    output_sum, input_sum = (
        lax.psum_scatter(output_part, "col", scatter_dimension=0, tiled=True),
        lax.psum_scatter(input_part, "col", scatter_dimension=0, tiled=True),
    )
    output = output_sum.astype(jnp.bfloat16)
    input_grad = input_sum.astype(jnp.bfloat16)
    gate_grad = tile_grads(whole_tokens, gate_all, gate_in, gate_out, gate_live, tile_size)
    up_grad = tile_grads(whole_tokens, up_all, up_in, up_out, up_live, tile_size)
    down_grad = tile_grads(hidden_all, whole_cotangent, down_in, down_out, down_live, tile_size)
    return (output, input_grad, gate_grad, up_grad, down_grad)


def solution(mesh):
    return jax.shard_map(
        body,
        mesh=mesh,
        in_specs=(
            P("col", "row"),
            P("col", "row"),
            P("row", "col", None),
            P("row", "col", None),
            P("row", "col", None),
            P(None, "row", "col"),
            P(None, "row", "col"),
        ),
        out_specs=(
            P("col", "row"),
            P("col", "row"),
            P("row", "col", None),
            P("row", "col", None),
            P("row", "col", None),
        ),
        check_vma=False,
    )
```

profile of v0, /device:TPU:0, one launch (start us, length us, event | category | flops | bytes accessed | tf_op | source)
XLA Modules:
  0.0 310.7 jit_solution(2265411004675898159)
XLA Ops:
  7.2 0.7 all-gather.5.cloned.1.call-update
  8.0 0.7 all-gather.7.cloned.1.call-update
  8.7 1.4 fusion.78
  10.7 0.8 slice_bitcast_fusion.5
  11.5 42.8 %all-gather.5.cloned.1.call-done = bf16[16,10,4096]{2,1,0:T(8,128)(2,1)} async-done(((bf16[1,10,4096]{2,1,0:T(8,128)(2,1)}), bf16[16,10,4096]{2,1,0:T(8,128)(2,1)}) %all-gather.5.cloned.1.call-update) | async-done | bytes 1310736 | tf_op jit(solution)/shard_map/all_gather | solution.py:70
  54.3 2.8 reshape.77
  57.7 0.8 fusion.13
  58.5 1.0 copy.109
  59.6 0.7 iota_compare_fusion.7
  60.8 0.8 fusion.15
  61.6 1.0 copy.110
  63.3 33.4 %all-gather.7.cloned.1.call-done = bf16[16,10,4096]{2,1,0:T(8,128)(2,1)} async-done(((bf16[1,10,4096]{2,1,0:T(8,128)(2,1)}), bf16[16,10,4096]{2,1,0:T(8,128)(2,1)}) %all-gather.7.cloned.1.call-update) | async-done | bytes 1310736 | tf_op jit(solution)/shard_map/all_gather | solution.py:71
  96.7 2.8 reshape.82
  100.7 0.7 fusion.9
  101.4 1.0 copy.108
  103.6 10.1 %reduce-scatter.6.cloned.1.call-done = f32[80,1024]{1,0:T(8,128)} async-done(((f32[160,1024]{1,0:T(8,128)}), f32[80,1024]{1,0:T(8,128)}) %reduce-scatter.6.cloned.1.call-update) | async-done | bytes 327696 | tf_op jit(solution)/shard_map/reduce_scatter | solution.py:80
  113.8 18.2 %reduce-scatter.4.cloned.1.call-done = f32[80,1024]{1,0:T(8,128)} async-done(((f32[160,1024]{1,0:T(8,128)}), f32[80,1024]{1,0:T(8,128)}) %reduce-scatter.4.cloned.1.call-update) | async-done | bytes 327696 | tf_op jit(solution)/shard_map/reduce_scatter | solution.py:79
  132.0 18.1 %reduce-scatter.8.cloned.1.call-done = f32[80,1024]{1,0:T(8,128)} async-done(((f32[160,1024]{1,0:T(8,128)}), f32[80,1024]{1,0:T(8,128)}) %reduce-scatter.8.cloned.1.call-update) | async-done | bytes 327696 | tf_op jit(solution)/shard_map/reduce_scatter | solution.py:81
  150.1 1.4 multiply_convert_fusion
  151.5 6.6 %all_gather.19 = bf16[160,1024]{1,0:T(8,128)(2,1)S(1)} all-gather(bf16[80,1024]{1,0:T(8,128)(2,1)S(1)} %get-tuple-element.7), channel_id=1, replica_groups=mesh['row'=2,'col'=16] {'row'}, dimensions={0}, use_global_device_ids=true | all-gather | bytes 491520 | tf_op jit(solution)/shard_map/all_gather | solution.py:87
  158.5 1.1 convolution_select_fusion.1
  159.8 6.0 %all_gather.18 = bf16[160,1024]{1,0:T(8,128)(2,1)S(1)} all-gather(bf16[80,1024]{1,0:T(8,128)(2,1)S(1)} %get-tuple-element.8), channel_id=1, replica_groups=mesh['row'=2,'col'=16] {'row'}, dimensions={0}, use_global_device_ids=true | all-gather | bytes 491520 | tf_op jit(solution)/shard_map/all_gather | solution.py:86
  166.1 1.1 convolution_select_fusion.2
  167.5 6.2 %all_gather.16 = bf16[160,1024]{1,0:T(8,128)(2,1)S(1)} all-gather(bf16[80,1024]{1,0:T(8,128)(2,1)S(1)} %get-tuple-element.9), channel_id=1, replica_groups=mesh['row'=2,'col'=16] {'row'}, dimensions={0}, use_global_device_ids=true | all-gather | bytes 491520 | tf_op jit(solution)/shard_map/all_gather | solution.py:85
  174.0 1.1 convolution_select_fusion
  175.3 1.4 fusion.11
  176.7 2.2 copy.107
  178.9 1.4 fusion.7
  180.2 1.5 convolution_add_fusion
  181.8 3.7 %copy.106 = f32[20,8,32,128]{3,1,2,0:T(8,128)} copy(f32[20,8,32,128]{3,2,1,0:T(8,128)S(1)} %bitcast.122) | data formatting | bytes 5242880
  185.5 117.0 %all-reduce.4 = (bf16[160,4096]{1,0:T(8,128)(2,1)}, bf16[160,4096]{1,0:T(8,128)(2,1)}) all-reduce(f32[160,4096]{1,0:T(8,128)S(1)} %bitcast.121, f32[160,4096]{1,0:T(8,128)} %bitcast.123), channel_id=4, replica_groups=mesh['row'=2,'col'=16] {'col'}, use_global_device_ids=true, to_apply=%region_2.0.clone | all-reduce | flops 1310720 | bytes 7864320
  302.4 1.8 dynamic-slice_convert_fusion
  (34 shorter events, 6.2 us)
Async XLA Ops:
  7.2 50.3 %copy-start = (bf16[6,128,128]{2,1,0:T(8,128)(2,1)S(1)}, bf16[6,128,128]{2,1,0:T(8,128)(2,1)}, u32[]{:S(2)}) copy-start(bf16[6,128,128]{2,1,0:T(8,128)(2,1)} %param.10) | copy-start | bytes 589828
  7.2 47.1 %all-gather.5.cloned.1.call-start = ((), (), s32[]{:S(2)}) async-start(), calls=%async_computation.6 | async-start | bytes 2228224 | tf_op jit(solution)/shard_map/all_gather | solution.py:70
  7.9 88.8 %all-gather.7.cloned.1.call-start = ((), (), s32[]{:S(2)}) async-start(), calls=%async_computation.7 | async-start | bytes 2228224 | tf_op jit(solution)/shard_map/all_gather | solution.py:71
  8.7 105.1 %reduce-scatter.6.cloned.1.call-start = ((), (), s32[]{:S(2)}) async-start(), calls=%async_computation.4 | async-start | bytes 983040 | tf_op jit(solution)/shard_map/reduce_scatter | solution.py:80
  59.5 1.1 copy-start.1
  59.5 72.5 %reduce-scatter.4.cloned.1.call-start = ((), (), s32[]{:S(2)}) async-start(), calls=%async_computation.3 | async-start | bytes 983040 | tf_op jit(solution)/shard_map/reduce_scatter | solution.py:79
  62.6 87.5 %reduce-scatter.8.cloned.1.call-start = ((), (), s32[]{:S(2)}) async-start(), calls=%async_computation.5 | async-start | bytes 983040 | tf_op jit(solution)/shard_map/reduce_scatter | solution.py:81
  99.5 0.9 copy-start.2
  101.4 1.0 copy-start.3
Sparse Core Ops, SparseCore 0:
  10.2 44.0 all-gather.4
  56.5 40.1 all-gather.6
  98.9 14.8 reduce-scatter.5
  116.0 15.9 reduce-scatter.3
  134.1 15.9 reduce-scatter.7
where the time goes:
time: 313 us; the launch traced here: 311 us
  blocking collectives  136 us (43%)
  waiting for transfers between devices  124 us (40%)
  local copies, waits for them, and re-layouts  19.7 us (6%)
  between operations  14.7 us (5%)
  matrix products  13.1 us (4%)
  other arithmetic  3.35 us (1%)
    unnamed x1, blocking collectives  117 us
    all_gather x1, waiting for transfers between devices, body(): lax.all_gather(tokens, 'col', axis=0, tiled=True)  42.8 us
    all_gather x1, waiting for transfers between devices, body(): lax.all_gather(cotangent, 'col', axis=0, tiled=True)  33.4 us
    reduce_scatter x1, waiting for transfers between devices, body(): lax.psum_scatter(gate_part, 'row', scatter_dimension=0, tiled=True)  18.2 us
    reduce_scatter x1, waiting for transfers between devices, body(): lax.psum_scatter(grad_part, 'row', scatter_dimension=0, tiled=True)  18.1 us
    reduce_scatter x1, waiting for transfers between devices, body(): lax.psum_scatter(up_part, 'row', scatter_dimension=0, tiled=True)  10.1 us
    unnamed x17, local copies, waits for them, and re-layouts  10.1 us
    all_gather x1, blocking collectives, body(): lax.all_gather(up_act, 'row', axis=0, tiled=True)  6.61 us
  transfers between devices with their start and end apart: 5, of which 5 were waited for; matrix products, arithmetic and copies ran while one was open for 6% of the time, Pallas kernels for 0%

commit v1 on v0

--- a/solution.py
+++ b/solution.py
@@ -1,6 +1,10 @@
+import functools
+
 import jax
 import jax.numpy as jnp
 from jax import lax
+from jax.experimental import pallas as pl
+from jax.experimental.pallas import tpu as pltpu
 from jax.sharding import PartitionSpec as P
 
 FF = 16384
@@ -55,7 +59,7 @@
     return (hidden, gate_act, up_act)
 
 
-def body(tokens, cotangent, gate_tiles, up_tiles, down_tiles, tile_index, tile_counts):
+def dense_body(tokens, cotangent, gate_tiles, up_tiles, down_tiles, tile_index, tile_counts):
     tile_size = gate_tiles.shape[-1]
     row_blocks = tokens.shape[1] // tile_size
     col_blocks = FF // lax.axis_size("col") // tile_size
@@ -103,7 +107,284 @@
     return (output, input_grad, gate_grad, up_grad, down_grad)
 
 
+MESH = pl.DeviceIdType.MESH
+F32 = jnp.float32
+BF16 = jnp.bfloat16
+NT = (((1,), (1,)), ((), ()))
+NN = (((1,), (0,)), ((), ()))
+TN = (((0,), (0,)), ((), ()))
+
+
+def dot(a, b, dims):
+    return lax.dot_general(a, b, dims, preferred_element_type=F32)
+
+
+def pair_at(matrix, slot, side, slots):
+    return (matrix * slots + slot) * 2 + side
+
+
+def exchange_kernel(
+    C, S, T, RB, CB, tile,
+    meta, tok, cot, gate_t, up_t, down_t,
+    got_out, meta_out, gate_g, up_g, down_g,
+    meta_v, meta_s, blocks, pack, send_a, recv_a, X, P, Pb, recv_b, acts, Q, send_c, recv_c,
+    m_send, m_recv, a_send, a_recv, b_send, b_recv, c_send, c_recv, local_sem,
+):
+    N = C * T
+    mc, mr = lax.axis_index("col"), lax.axis_index("row")
+    partner = 1 - mr
+    tiles = (gate_t, up_t, down_t)
+    grads = (gate_g, up_g, down_g)
+    n_meta = 3 * S * 2
+
+    barrier = pltpu.get_barrier_semaphore()
+
+    def greet(k, _):
+        pl.semaphore_signal(barrier, inc=1, device_id={"col": lax.rem(mc + k, C)}, device_id_type=MESH)
+        return 0
+
+    lax.fori_loop(1, C, greet, 0)
+    pl.semaphore_signal(barrier, inc=1, device_id={"row": partner}, device_id_type=MESH)
+    pl.semaphore_wait(barrier, C)
+
+    def meta_copy(k, owner, target):
+        return pltpu.make_async_remote_copy(
+            src_ref=meta, dst_ref=meta_v.at[owner], send_sem=m_send.at[k], recv_sem=m_recv.at[k],
+            device_id={"col": target}, device_id_type=MESH,
+        )
+
+    def meta_row(owner):
+        return pltpu.make_async_remote_copy(
+            src_ref=meta, dst_ref=meta_v.at[C + owner], send_sem=m_send.at[0], recv_sem=m_recv.at[0],
+            device_id={"row": partner}, device_id_type=MESH,
+        )
+
+    def meta_start(k, _):
+        meta_copy(k, mc, lax.rem(mc + k, C)).start()
+        return 0
+
+    lax.fori_loop(1, C, meta_start, 0)
+    meta_row(mr).start()
+    meta_v[mc] = meta[...]
+    meta_v[C + mr] = meta[...]
+    for b in range(RB):
+        blocks[b, 0:T, :] = tok[:, b * tile:(b + 1) * tile].astype(F32)
+        blocks[RB + b, 0:T, :] = cot[:, b * tile:(b + 1) * tile].astype(F32)
+    pack[...] = jnp.zeros_like(pack)
+
+    def meta_wait(k, _):
+        meta_copy(k, lax.rem(mc - k + C, C), lax.rem(mc + k, C)).wait()
+        return 0
+
+    lax.fori_loop(1, C, meta_wait, 0)
+    meta_row(partner).wait()
+    to_smem = pltpu.make_async_copy(meta_v, meta_s, local_sem)
+    to_smem.start()
+    to_smem.wait()
+
+    def a_copy(k, owner, target):
+        return pltpu.make_async_remote_copy(
+            src_ref=send_a.at[k], dst_ref=recv_a.at[owner], send_sem=a_send.at[k], recv_sem=a_recv.at[k],
+            device_id={"col": target}, device_id_type=MESH,
+        )
+
+    def pick_for(dest):
+        for s in range(3 * S):
+            m = s // S
+            side, base = (1, RB) if m == 2 else (0, 0)
+            b = meta_s[dest, 0, pair_at(m, s % S, side, S)] + base
+            pack[s * T:(s + 1) * T, :] = blocks[b, 0:T, :]
+
+    def a_start(k, _):
+        dest = lax.rem(mc + k, C)
+        pick_for(dest)
+        send_a[k] = pack[...].astype(BF16)
+        a_copy(k, mc, dest).start()
+        return 0
+
+    lax.fori_loop(1, C, a_start, 0)
+    pick_for(mc)
+    for s in range(3 * S):
+        X[s, 0:T, :] = pack[s * T:(s + 1) * T, :]
+
+    def a_wait(k, _):
+        src = lax.rem(mc - k + C, C)
+        a_copy(k, src, lax.rem(mc + k, C)).wait()
+        pack[...] = recv_a[src].astype(F32)
+        for s in range(3 * S):
+            X[s, pl.ds(k * T, T), :] = pack[s * T:(s + 1) * T, :]
+        return 0
+
+    lax.fori_loop(1, C, a_wait, 0)
+
+    def live(m, s):
+        return s < meta_s[mc, 0, n_meta + m]
+
+    def b_copy(m):
+        return pltpu.make_async_remote_copy(
+            src_ref=Pb.at[m], dst_ref=recv_b.at[m], send_sem=b_send.at[m], recv_sem=b_recv.at[m],
+            device_id={"row": partner}, device_id_type=MESH,
+        )
+
+    for m in range(3):
+        def product(s, _, m=m):
+            part = dot(X[m * S + s].astype(BF16), tiles[m][s], NT if m == 2 else NN)
+            part = jnp.where(live(m, s), part, 0.0)
+            P[m * S + s] = part
+            Pb[m, s] = part.astype(BF16)
+            return 0
+
+        lax.fori_loop(0, S, product, 0)
+        b_copy(m).start()
+    for m in range(3):
+        b_copy(m).wait()
+
+    step = N // 2 if N % 32 == 0 else N
+
+    def activate(j, _):
+        for half in range(N // step):
+            rows = slice(half * step, (half + 1) * step)
+            sums = []
+            for m in range(3):
+                side = 0 if m == 2 else 1
+                total = jnp.zeros((step, tile), F32)
+                for s in range(S):
+                    at = pair_at(m, s, side, S)
+                    total = total + jnp.where(meta_s[mc, 0, at] == j, P[m * S + s, rows, :], 0.0)
+                    total = total + jnp.where(
+                        meta_s[C + partner, 0, at] == j, recv_b[m, s, rows, :].astype(F32), 0.0
+                    )
+                sums.append(total)
+            g, u, hg = sums
+            sg = jax.nn.sigmoid(g)
+            active = g * sg
+            acts[0, j, rows, :] = (hg * u * sg * (1.0 + g * (1.0 - sg))).astype(BF16)
+            acts[1, j, rows, :] = (hg * active).astype(BF16)
+            acts[2, j, rows, :] = (active * u).astype(BF16)
+        return 0
+
+    lax.fori_loop(0, CB, activate, 0)
+
+    for m in range(3):
+        def back(s, _, m=m):
+            j = meta_s[mc, 0, pair_at(m, s, 0 if m == 2 else 1, S)]
+            part = dot(acts[m, j], tiles[m][s], NN if m == 2 else NT)
+            Q[m * S + s] = jnp.where(live(m, s), part, 0.0)
+            return 0
+
+        lax.fori_loop(0, S, back, 0)
+
+    def c_copy(k, owner, target):
+        return pltpu.make_async_remote_copy(
+            src_ref=send_c.at[k], dst_ref=recv_c.at[owner], send_sem=c_send.at[k], recv_sem=c_recv.at[k],
+            device_id={"col": target}, device_id_type=MESH,
+        )
+
+    def c_start(k, _):
+        for s in range(3 * S):
+            pack[s * T:(s + 1) * T, :] = Q[s, pl.ds(k * T, T), :]
+        send_c[k] = pack[...].astype(BF16)
+        c_copy(k, mc, lax.rem(mc - k + C, C)).start()
+        return 0
+
+    lax.fori_loop(1, C, c_start, 0)
+    for s in range(3 * S):
+        pack[s * T:(s + 1) * T, :] = Q[s, 0:T, :]
+    got_out[mc] = pack[...].astype(BF16)
+    meta_out[...] = meta_v[...]
+
+    for m in range(3):
+        def tile_grad(s, _, m=m):
+            j = meta_s[mc, 0, pair_at(m, s, 0 if m == 2 else 1, S)]
+            x = X[m * S + s].astype(BF16)
+            part = dot(acts[m, j], x, TN) if m == 2 else dot(x, acts[m, j], TN)
+            grads[m][s] = jnp.where(live(m, s), part, 0.0)
+            return 0
+
+        lax.fori_loop(0, S, tile_grad, 0)
+
+    def c_wait(k, _):
+        src = lax.rem(mc + k, C)
+        c_copy(k, src, lax.rem(mc - k + C, C)).wait()
+        got_out[src] = recv_c[src]
+        return 0
+
+    lax.fori_loop(1, C, c_wait, 0)
+
+
+def add_kernel(C, S, T, RB, tile, meta, got, out, ingrad, total, pack):
+    total[...] = jnp.zeros_like(total)
+
+    def add(c, _):
+        pack[...] = got[c].astype(F32)
+        for s in range(3 * S):
+            m = s // S
+            side, base = (1, RB) if m == 2 else (0, 0)
+            b = meta[c, 0, pair_at(m, s % S, side, S)] + base
+            total[b, 0:T, :] += pack[s * T:(s + 1) * T, :]
+        return 0
+
+    lax.fori_loop(0, C, add, 0)
+    for b in range(RB):
+        ingrad[:, b * tile:(b + 1) * tile] = total[b, 0:T, :].astype(BF16)
+        out[:, b * tile:(b + 1) * tile] = total[RB + b, 0:T, :].astype(BF16)
+
+
+def sparse_body(tokens, cotangent, gate_tiles, up_tiles, down_tiles, tile_index, tile_counts):
+    C, R = lax.axis_size("col"), lax.axis_size("row")
+    T, width = tokens.shape
+    S, tile = gate_tiles.shape[0], gate_tiles.shape[-1]
+    RB, CB = width // tile, FF // C // tile
+    N = C * T
+    rows = -(-3 * S * T // 16) * 16
+    pad_t = -(-T // 8) * 8
+    meta = jnp.concatenate([tile_index.reshape(-1), tile_counts.reshape(-1)])
+    meta = jnp.pad(meta, (0, 1024 - meta.shape[0])).reshape(8, 128)
+    V, M = pltpu.VMEM, pltpu.SemaphoreType.DMA
+    vspec = pl.BlockSpec(memory_space=pltpu.VMEM)
+    sd = jax.ShapeDtypeStruct
+    got, metas, gate_grad, up_grad, down_grad = pl.pallas_call(
+        functools.partial(exchange_kernel, C, S, T, RB, CB, tile),
+        out_shape=[sd((C, rows, tile), BF16), sd((C + R, 8, 128), jnp.int32)]
+        + [sd((S, tile, tile), F32)] * 3,
+        in_specs=[vspec] * 6,
+        out_specs=[vspec] * 5,
+        scratch_shapes=[
+            V((C + R, 8, 128), jnp.int32),
+            pltpu.SMEM((C + R, 8, 128), jnp.int32),
+            V((2 * RB, pad_t, tile), F32),
+            V((rows, tile), F32),
+            V((C, rows, tile), BF16),
+            V((C, rows, tile), BF16),
+            V((3 * S, N, tile), F32),
+            V((3 * S, N, tile), F32),
+            V((3, S, N, tile), BF16),
+            V((3, S, N, tile), BF16),
+            V((3, CB, N, tile), BF16),
+            V((3 * S, N, tile), F32),
+            V((C, rows, tile), BF16),
+            V((C, rows, tile), BF16),
+            M((C,)), M((C,)), M((C,)), M((C,)), M((3,)), M((3,)), M((C,)), M((C,)), M,
+        ],
+        compiler_params=pltpu.CompilerParams(
+            collective_id=0, has_side_effects=True, vmem_limit_bytes=40 * 1024 * 1024
+        ),
+        name="exchange",
+    )(meta, tokens, cotangent, gate_tiles, up_tiles, down_tiles)
+    output, input_grad = pl.pallas_call(
+        functools.partial(add_kernel, C, S, T, RB, tile),
+        out_shape=[sd((T, width), BF16)] * 2,
+        in_specs=[pl.BlockSpec(memory_space=pltpu.SMEM), vspec],
+        out_specs=[vspec] * 2,
+        scratch_shapes=[V((2 * RB, pad_t, tile), F32), V((rows, tile), F32)],
+        compiler_params=pltpu.CompilerParams(vmem_limit_bytes=16 * 1024 * 1024),
+        name="add_slots",
+    )(metas, got)
+    return (output, input_grad, gate_grad, up_grad, down_grad)
+
+
 def solution(mesh):
+    body = sparse_body if mesh.shape["row"] == 2 else dense_body
     return jax.shard_map(
         body,
         mesh=mesh,

time: 313 us -> 85.3 us (0.27)
  blocking collectives: 136 us -> 0 us
  waiting for transfers between devices: 124 us -> 0 us
  Pallas kernels: 0 us -> 76 us
  between operations: 14.7 us -> 0.65 us
  matrix products: 13.1 us -> 0 us
  local copies, waits for them, and re-layouts: 19.7 us -> 8.26 us
  other arithmetic: 3.35 us -> 0.07 us
    unnamed x1 -> x0, blocking collectives: 117 us -> none
    all_gather x2 -> x0, waiting for transfers between devices: 76.2 us -> none  [the longest x1 42.8 us: body(): lax.all_gather(tokens, 'col', axis=0, tiled=True)]
    pallas_call x0 -> x2, Pallas kernels: none -> 76 us  [the longest x1 72.4 us: sparse_body(): pl.pallas_call(functools.partial(exchange_kernel, C, S, T, RB, CB, tile),...]
    reduce_scatter x3 -> x0, waiting for transfers between devices: 46.5 us -> none  [the longest x1 18.2 us: body(): lax.psum_scatter(gate_part, 'row', scatter_dimension=0, tiled=True)]
    all_gather x3 -> x0, blocking collectives: 18.8 us -> none  [the longest x1 6.61 us: body(): lax.all_gather(up_act, 'row', axis=0, tiled=True)]
    dot_general x21 -> x0, matrix products: 13.1 us -> none  [the longest x6 6.57 us: place_blocks(): jnp.einsum('tsn,sc->tcn', products, select, precision=lax.Precision.HIGHEST)]
    reshape x2, local copies, waits for them, and re-layouts: 5.63 us -> 0.09 us  [the longest x1 0.09 us: sparse_body(): meta = jnp.concatenate([tile_index.reshape(-1), tile_counts.reshape(-1)])]
    unnamed x17 -> x16, local copies, waits for them, and re-layouts: 10.1 us -> 8.17 us
  transfers between devices with their start and end apart: 5 -> 0, of which waited for: 5 -> 0; matrix products, arithmetic and copies ran while one was open for 6% -> 0% of each run, Pallas kernels for 0% -> 0%
where the time goes in v1:
time: 85.3 us; the launch traced here: 85 us
  Pallas kernels  76 us (89%)
  local copies, waits for them, and re-layouts  8.26 us (10%)
    pallas_call x1, Pallas kernels, sparse_body(): pl.pallas_call(functools.partial(exchange_kernel, C, S, T, RB, CB, tile),...  72.4 us
    unnamed x16, local copies, waits for them, and re-layouts  8.17 us
    pallas_call x1, Pallas kernels, sparse_body(): pl.pallas_call(functools.partial(add_kernel, C, S, T, RB, tile), out_shap...  3.64 us

profile of v1, /device:TPU:0, one launch (start us, length us, event | category | flops | bytes accessed | tf_op | source)
XLA Modules:
  0.0 85.0 jit_solution(10956893288333246084)
XLA Ops:
  0.6 0.8 copy.13
  1.4 0.0 copy-start.5
  1.4 0.1 reshape.19
  1.5 0.6 copy-done.5
  2.1 0.1 pad_add_fusion
  2.2 0.0 copy-start
  2.2 0.9 %copy-done = bf16[6,128,128]{2,1,0:T(8,128)(2,1)S(1)} copy-done((bf16[6,128,128]{2,1,0:T(8,128)(2,1)S(1)}, bf16[6,128,128]{2,1,0:T(8,128)(2,1)}, u32[]{:S(2)}) %copy-start) | copy-done | bytes 196632
  3.1 0.0 copy-start.1
  3.1 0.9 %copy-done.1 = bf16[6,128,128]{2,1,0:T(8,128)(2,1)S(1)} copy-done((bf16[6,128,128]{2,1,0:T(8,128)(2,1)S(1)}, bf16[6,128,128]{2,1,0:T(8,128)(2,1)}, u32[]{:S(2)}) %copy-start.1) | copy-done | bytes 196632
  4.0 0.0 copy-start.2
  4.0 0.9 %copy-done.2 = bf16[6,128,128]{2,1,0:T(8,128)(2,1)S(1)} copy-done((bf16[6,128,128]{2,1,0:T(8,128)(2,1)S(1)}, bf16[6,128,128]{2,1,0:T(8,128)(2,1)}, u32[]{:S(2)}) %copy-start.2) | copy-done | bytes 196632
  4.9 0.0 copy-start.3
  4.9 0.9 %copy-done.3 = bf16[10,4096]{1,0:T(8,128)(2,1)S(1)} copy-done((bf16[10,4096]{1,0:T(8,128)(2,1)S(1)}, bf16[10,4096]{1,0:T(8,128)(2,1)}, u32[]{:S(2)}) %copy-start.3) | copy-done | bytes 81944
  5.8 0.0 copy-start.4
  5.8 0.9 %copy-done.4 = bf16[10,4096]{1,0:T(8,128)(2,1)S(1)} copy-done((bf16[10,4096]{1,0:T(8,128)(2,1)S(1)}, bf16[10,4096]{1,0:T(8,128)(2,1)}, u32[]{:S(2)}) %copy-start.4) | copy-done | bytes 81944
  6.7 72.4 %exchange.1 = (bf16[16,192,128]{2,1,0:T(8,128)(2,1)S(1)}, s32[18,8,128]{2,1,0:T(8,128)S(1)}, f32[6,128,128]{2,1,0:T(8,128)S(1)}, f32[6,128,128]{2,1,0:T(8,128)S(1)}, f32[6,128,128]{2,1,0:T(8,128)S(1)}) custom-call(s32[8,128]{1,0:T(8,128)S(1)} %pad_bitcast_fusion.meta, bf16[10,4096]{1,0:T(8,128)(2,1)S(1)} %copy-done.3, bf16[10,4096]{1,0:T(8,128)(2,1)S(1)} %copy-done.4, ...), custom_call_target="tpu_custom_call" | custom-call | tf_op jit(solution)/shard_map/exchange/pallas_call | solution.py:346
  79.1 3.6 %add_slots.1 = (bf16[10,4096]{1,0:T(8,128)(2,1)}, bf16[10,4096]{1,0:T(8,128)(2,1)}) custom-call(s32[18,8,128]{2,1,0:T(8,128)S(1)} %get-tuple-element.12.meta, bf16[16,192,128]{2,1,0:T(8,128)(2,1)S(1)} %get-tuple-element.13.got), custom_call_target="tpu_custom_call" | custom-call | tf_op jit(solution)/shard_map/add_slots/pallas_call | solution.py:374
  82.8 0.7 copy.17
  83.5 0.7 copy.18
  84.3 0.7 copy.19
  (1 shorter events, 0.0 us)
Async XLA Ops:
  1.4 0.7 copy-start.5
  2.2 0.9 %copy-start = (bf16[6,128,128]{2,1,0:T(8,128)(2,1)S(1)}, bf16[6,128,128]{2,1,0:T(8,128)(2,1)}, u32[]{:S(2)}) copy-start(bf16[6,128,128]{2,1,0:T(8,128)(2,1)} %gate_t.1) | copy-start | bytes 589828
  3.1 0.9 %copy-start.1 = (bf16[6,128,128]{2,1,0:T(8,128)(2,1)S(1)}, bf16[6,128,128]{2,1,0:T(8,128)(2,1)}, u32[]{:S(2)}) copy-start(bf16[6,128,128]{2,1,0:T(8,128)(2,1)} %up_t.1) | copy-start | bytes 589828
  4.0 0.9 %copy-start.2 = (bf16[6,128,128]{2,1,0:T(8,128)(2,1)S(1)}, bf16[6,128,128]{2,1,0:T(8,128)(2,1)}, u32[]{:S(2)}) copy-start(bf16[6,128,128]{2,1,0:T(8,128)(2,1)} %down_t.1) | copy-start | bytes 589828
  4.9 0.9 %copy-start.3 = (bf16[10,4096]{1,0:T(8,128)(2,1)S(1)}, bf16[10,4096]{1,0:T(8,128)(2,1)}, u32[]{:S(2)}) copy-start(bf16[10,4096]{1,0:T(8,128)(2,1)} %tok.1) | copy-start | bytes 245764
  5.8 0.9 %copy-start.4 = (bf16[10,4096]{1,0:T(8,128)(2,1)S(1)}, bf16[10,4096]{1,0:T(8,128)(2,1)}, u32[]{:S(2)}) copy-start(bf16[10,4096]{1,0:T(8,128)(2,1)} %cot.1) | copy-start | bytes 245764

commit v2 on v1

--- a/solution.py
+++ b/solution.py
@@ -119,23 +119,32 @@
     return lax.dot_general(a, b, dims, preferred_element_type=F32)
 
 
-def pair_at(matrix, slot, side, slots):
-    return (matrix * slots + slot) * 2 + side
-
-
 def exchange_kernel(
-    C, S, T, RB, CB, tile,
-    meta, tok, cot, gate_t, up_t, down_t,
+    C, S, T, RB, CB, tile, G,
+    index, counts, tok, cot, gate_t, up_t, down_t,
     got_out, meta_out, gate_g, up_g, down_g,
+    index_v, counts_v, meta, tiles_v, grads_v,
     meta_v, meta_s, blocks, pack, send_a, recv_a, X, P, Pb, recv_b, acts, Q, send_c, recv_c,
-    m_send, m_recv, a_send, a_recv, b_send, b_recv, c_send, c_recv, local_sem,
+    m_send, m_recv, a_send, a_recv, b_send, b_recv, c_send, c_recv, in_sem, out_sem, local_sem,
 ):
     N = C * T
+    H, peers = N // G, C // G
     mc, mr = lax.axis_index("col"), lax.axis_index("row")
     partner = 1 - mr
-    tiles = (gate_t, up_t, down_t)
-    grads = (gate_g, up_g, down_g)
-    n_meta = 3 * S * 2
+    index_copy = pltpu.make_async_copy(index, index_v, in_sem.at[3])
+    counts_copy = pltpu.make_async_copy(counts, counts_v, in_sem.at[4])
+    tile_copies = [
+        pltpu.make_async_copy(ref, tiles_v.at[m], in_sem.at[m])
+        for m, ref in enumerate((gate_t, up_t, down_t))
+    ]
+    grad_copies = [
+        pltpu.make_async_copy(grads_v.at[m], ref, out_sem.at[m])
+        for m, ref in enumerate((gate_g, up_g, down_g))
+    ]
+    index_copy.start()
+    counts_copy.start()
+    for copy in tile_copies:
+        copy.start()
 
     barrier = pltpu.get_barrier_semaphore()
 
@@ -145,6 +154,12 @@
 
     lax.fori_loop(1, C, greet, 0)
     pl.semaphore_signal(barrier, inc=1, device_id={"row": partner}, device_id_type=MESH)
+    index_copy.wait()
+    counts_copy.wait()
+    meta[...] = jnp.zeros_like(meta)
+    for m in range(3):
+        meta[0:S, 2 * m:2 * m + 2] = index_v[m]
+        meta[S:S + 1, m:m + 1] = counts_v[m]
     pl.semaphore_wait(barrier, C)
 
     def meta_copy(k, owner, target):
@@ -192,7 +207,7 @@
         for s in range(3 * S):
             m = s // S
             side, base = (1, RB) if m == 2 else (0, 0)
-            b = meta_s[dest, 0, pair_at(m, s % S, side, S)] + base
+            b = meta_s[dest, s % S, 2 * m + side] + base
             pack[s * T:(s + 1) * T, :] = blocks[b, 0:T, :]
 
     def a_start(k, _):
@@ -215,64 +230,32 @@
             X[s, pl.ds(k * T, T), :] = pack[s * T:(s + 1) * T, :]
         return 0
 
-    lax.fori_loop(1, C, a_wait, 0)
-
     def live(m, s):
-        return s < meta_s[mc, 0, n_meta + m]
-
-    def b_copy(m):
+        return s < meta_s[mc, S, m]
+
+    def b_copy(g, m):
         return pltpu.make_async_remote_copy(
-            src_ref=Pb.at[m], dst_ref=recv_b.at[m], send_sem=b_send.at[m], recv_sem=b_recv.at[m],
+            src_ref=Pb.at[g, m], dst_ref=recv_b.at[g, m],
+            send_sem=b_send.at[g, m], recv_sem=b_recv.at[g, m],
             device_id={"row": partner}, device_id_type=MESH,
         )
 
-    for m in range(3):
-        def product(s, _, m=m):
-            part = dot(X[m * S + s].astype(BF16), tiles[m][s], NT if m == 2 else NN)
-            part = jnp.where(live(m, s), part, 0.0)
-            P[m * S + s] = part
-            Pb[m, s] = part.astype(BF16)
-            return 0
-
-        lax.fori_loop(0, S, product, 0)
-        b_copy(m).start()
-    for m in range(3):
-        b_copy(m).wait()
-
-    step = N // 2 if N % 32 == 0 else N
-
-    def activate(j, _):
-        for half in range(N // step):
-            rows = slice(half * step, (half + 1) * step)
-            sums = []
-            for m in range(3):
-                side = 0 if m == 2 else 1
-                total = jnp.zeros((step, tile), F32)
-                for s in range(S):
-                    at = pair_at(m, s, side, S)
-                    total = total + jnp.where(meta_s[mc, 0, at] == j, P[m * S + s, rows, :], 0.0)
-                    total = total + jnp.where(
-                        meta_s[C + partner, 0, at] == j, recv_b[m, s, rows, :].astype(F32), 0.0
-                    )
-                sums.append(total)
-            g, u, hg = sums
-            sg = jax.nn.sigmoid(g)
-            active = g * sg
-            acts[0, j, rows, :] = (hg * u * sg * (1.0 + g * (1.0 - sg))).astype(BF16)
-            acts[1, j, rows, :] = (hg * active).astype(BF16)
-            acts[2, j, rows, :] = (active * u).astype(BF16)
-        return 0
-
-    lax.fori_loop(0, CB, activate, 0)
-
-    for m in range(3):
-        def back(s, _, m=m):
-            j = meta_s[mc, 0, pair_at(m, s, 0 if m == 2 else 1, S)]
-            part = dot(acts[m, j], tiles[m][s], NN if m == 2 else NT)
-            Q[m * S + s] = jnp.where(live(m, s), part, 0.0)
-            return 0
-
-        lax.fori_loop(0, S, back, 0)
+    for g in range(G):
+        rows = slice(g * H, (g + 1) * H)
+        lax.fori_loop(max(1, g * peers), (g + 1) * peers, a_wait, 0)
+        if g == 0:
+            for copy in tile_copies:
+                copy.wait()
+        for m in range(3):
+            def product(s, _, m=m, g=g, rows=rows):
+                part = dot(X[m * S + s, rows, :].astype(BF16), tiles_v[m, s], NT if m == 2 else NN)
+                part = jnp.where(live(m, s), part, 0.0)
+                P[m * S + s, rows, :] = part
+                Pb[g, m, s] = part.astype(BF16)
+                return 0
+
+            lax.fori_loop(0, S, product, 0)
+            b_copy(g, m).start()
 
     def c_copy(k, owner, target):
         return pltpu.make_async_remote_copy(
@@ -287,7 +270,42 @@
         c_copy(k, mc, lax.rem(mc - k + C, C)).start()
         return 0
 
-    lax.fori_loop(1, C, c_start, 0)
+    for g in range(G):
+        rows = slice(g * H, (g + 1) * H)
+        for m in range(3):
+            b_copy(g, m).wait()
+
+        def activate(j, _, g=g, rows=rows):
+            sums = []
+            for m in range(3):
+                side = 0 if m == 2 else 1
+                total = jnp.zeros((H, tile), F32)
+                for s in range(S):
+                    mine = meta_s[mc, s, 2 * m + side] == j
+                    theirs = meta_s[C + partner, s, 2 * m + side] == j
+                    total = total + jnp.where(mine, P[m * S + s, rows, :], 0.0)
+                    total = total + jnp.where(theirs, recv_b[g, m, s].astype(F32), 0.0)
+                sums.append(total)
+            gate, up, hg = sums
+            sg = jax.nn.sigmoid(gate)
+            active = gate * sg
+            acts[0, j, rows, :] = (hg * up * sg * (1.0 + gate * (1.0 - sg))).astype(BF16)
+            acts[1, j, rows, :] = (hg * active).astype(BF16)
+            acts[2, j, rows, :] = (active * up).astype(BF16)
+            return 0
+
+        lax.fori_loop(0, CB, activate, 0)
+
+        for m in range(3):
+            def back(s, _, m=m, rows=rows):
+                j = meta_s[mc, s, 2 * m + (0 if m == 2 else 1)]
+                part = dot(acts[m, j, rows, :], tiles_v[m, s], NN if m == 2 else NT)
+                Q[m * S + s, rows, :] = jnp.where(live(m, s), part, 0.0)
+                return 0
+
+            lax.fori_loop(0, S, back, 0)
+        lax.fori_loop(max(1, g * peers), (g + 1) * peers, c_start, 0)
+
     for s in range(3 * S):
         pack[s * T:(s + 1) * T, :] = Q[s, 0:T, :]
     got_out[mc] = pack[...].astype(BF16)
@@ -295,13 +313,14 @@
 
     for m in range(3):
         def tile_grad(s, _, m=m):
-            j = meta_s[mc, 0, pair_at(m, s, 0 if m == 2 else 1, S)]
+            j = meta_s[mc, s, 2 * m + (0 if m == 2 else 1)]
             x = X[m * S + s].astype(BF16)
             part = dot(acts[m, j], x, TN) if m == 2 else dot(x, acts[m, j], TN)
-            grads[m][s] = jnp.where(live(m, s), part, 0.0)
+            grads_v[m, s] = jnp.where(live(m, s), part, 0.0)
             return 0
 
         lax.fori_loop(0, S, tile_grad, 0)
+        grad_copies[m].start()
 
     def c_wait(k, _):
         src = lax.rem(mc + k, C)
@@ -310,9 +329,20 @@
         return 0
 
     lax.fori_loop(1, C, c_wait, 0)
-
-
-def add_kernel(C, S, T, RB, tile, meta, got, out, ingrad, total, pack):
+    for copy in grad_copies:
+        copy.wait()
+
+
+def add_kernel(
+    C, S, T, RB, tile, meta, got, gate_in, up_in, down_in,
+    out, ingrad, gate_g, up_g, down_g, total, pack, sem,
+):
+    copies = [
+        pltpu.make_async_copy(src, dst, sem.at[m])
+        for m, (src, dst) in enumerate(((gate_in, gate_g), (up_in, up_g), (down_in, down_g)))
+    ]
+    for copy in copies:
+        copy.start()
     total[...] = jnp.zeros_like(total)
 
     def add(c, _):
@@ -320,7 +350,7 @@
         for s in range(3 * S):
             m = s // S
             side, base = (1, RB) if m == 2 else (0, 0)
-            b = meta[c, 0, pair_at(m, s % S, side, S)] + base
+            b = meta[c, s % S, 2 * m + side] + base
             total[b, 0:T, :] += pack[s * T:(s + 1) * T, :]
         return 0
 
@@ -328,6 +358,8 @@
     for b in range(RB):
         ingrad[:, b * tile:(b + 1) * tile] = total[b, 0:T, :].astype(BF16)
         out[:, b * tile:(b + 1) * tile] = total[RB + b, 0:T, :].astype(BF16)
+    for copy in copies:
+        copy.wait()
 
 
 def sparse_body(tokens, cotangent, gate_tiles, up_tiles, down_tiles, tile_index, tile_counts):
@@ -338,49 +370,56 @@
     N = C * T
     rows = -(-3 * S * T // 16) * 16
     pad_t = -(-T // 8) * 8
-    meta = jnp.concatenate([tile_index.reshape(-1), tile_counts.reshape(-1)])
-    meta = jnp.pad(meta, (0, 1024 - meta.shape[0])).reshape(8, 128)
+    G = 2 if C % 2 == 0 and (N // 2) % 16 == 0 else 1
+    H = N // G
+    meta_rows = -(-(S + 1) // 8) * 8
     V, M = pltpu.VMEM, pltpu.SemaphoreType.DMA
     vspec = pl.BlockSpec(memory_space=pltpu.VMEM)
+    hbm = pl.BlockSpec(memory_space=pl.ANY)
     sd = jax.ShapeDtypeStruct
     got, metas, gate_grad, up_grad, down_grad = pl.pallas_call(
-        functools.partial(exchange_kernel, C, S, T, RB, CB, tile),
-        out_shape=[sd((C, rows, tile), BF16), sd((C + R, 8, 128), jnp.int32)]
+        functools.partial(exchange_kernel, C, S, T, RB, CB, tile, G),
+        out_shape=[sd((C, rows, tile), BF16), sd((C + R, meta_rows, 128), jnp.int32)]
         + [sd((S, tile, tile), F32)] * 3,
-        in_specs=[vspec] * 6,
-        out_specs=[vspec] * 5,
+        in_specs=[hbm] * 2 + [vspec] * 2 + [hbm] * 3,
+        out_specs=[vspec] * 2 + [hbm] * 3,
         scratch_shapes=[
-            V((C + R, 8, 128), jnp.int32),
-            pltpu.SMEM((C + R, 8, 128), jnp.int32),
+            V(tile_index.shape, jnp.int32),
+            V(tile_counts.shape, jnp.int32),
+            V((meta_rows, 128), jnp.int32),
+            V((3, S, tile, tile), BF16),
+            V((3, S, tile, tile), F32),
+            V((C + R, meta_rows, 128), jnp.int32),
+            pltpu.SMEM((C + R, meta_rows, 128), jnp.int32),
             V((2 * RB, pad_t, tile), F32),
             V((rows, tile), F32),
             V((C, rows, tile), BF16),
             V((C, rows, tile), BF16),
             V((3 * S, N, tile), F32),
             V((3 * S, N, tile), F32),
-            V((3, S, N, tile), BF16),
-            V((3, S, N, tile), BF16),
+            V((G, 3, S, H, tile), BF16),
+            V((G, 3, S, H, tile), BF16),
             V((3, CB, N, tile), BF16),
             V((3 * S, N, tile), F32),
             V((C, rows, tile), BF16),
             V((C, rows, tile), BF16),
-            M((C,)), M((C,)), M((C,)), M((C,)), M((3,)), M((3,)), M((C,)), M((C,)), M,
+            M((C,)), M((C,)), M((C,)), M((C,)), M((G, 3)), M((G, 3)), M((C,)), M((C,)),
+            M((5,)), M((3,)), M,
         ],
         compiler_params=pltpu.CompilerParams(
             collective_id=0, has_side_effects=True, vmem_limit_bytes=40 * 1024 * 1024
         ),
         name="exchange",
-    )(meta, tokens, cotangent, gate_tiles, up_tiles, down_tiles)
-    output, input_grad = pl.pallas_call(
+    )(tile_index, tile_counts, tokens, cotangent, gate_tiles, up_tiles, down_tiles)
+    return pl.pallas_call(
         functools.partial(add_kernel, C, S, T, RB, tile),
-        out_shape=[sd((T, width), BF16)] * 2,
-        in_specs=[pl.BlockSpec(memory_space=pltpu.SMEM), vspec],
-        out_specs=[vspec] * 2,
-        scratch_shapes=[V((2 * RB, pad_t, tile), F32), V((rows, tile), F32)],
+        out_shape=[sd((T, width), BF16)] * 2 + [sd((S, tile, tile), F32)] * 3,
+        in_specs=[pl.BlockSpec(memory_space=pltpu.SMEM), vspec] + [hbm] * 3,
+        out_specs=[vspec] * 2 + [hbm] * 3,
+        scratch_shapes=[V((2 * RB, pad_t, tile), F32), V((rows, tile), F32), M((3,))],
         compiler_params=pltpu.CompilerParams(vmem_limit_bytes=16 * 1024 * 1024),
         name="add_slots",
-    )(metas, got)
-    return (output, input_grad, gate_grad, up_grad, down_grad)
+    )(metas, got, gate_grad, up_grad, down_grad)
 
 
 def solution(mesh):

time: 85.3 us -> 73 us (0.86)
  Pallas kernels: 76 us -> 66 us
  local copies, waits for them, and re-layouts: 8.26 us -> 6.11 us
    pallas_call x1, Pallas kernels: 72.4 us -> 62.5 us  [sparse_body(): pl.pallas_call(functools.partial(exchange_kernel, C, S, T, RB, CB, tile,...]
    unnamed x16 -> x12, local copies, waits for them, and re-layouts: 8.17 us -> 6.11 us
where the time goes in v2:
time: 73 us; the launch traced here: 72.8 us
  Pallas kernels  66 us (90%)
  local copies, waits for them, and re-layouts  6.11 us (8%)
    pallas_call x1, Pallas kernels, sparse_body(): pl.pallas_call(functools.partial(exchange_kernel, C, S, T, RB, CB, tile,...  62.5 us
    unnamed x12, local copies, waits for them, and re-layouts  6.11 us
    pallas_call x1, Pallas kernels, sparse_body(): pl.pallas_call(functools.partial(add_kernel, C, S, T, RB, tile), out_shap...  3.47 us

profile of v2, /device:TPU:0, one launch (start us, length us, event | category | flops | bytes accessed | tf_op | source)
XLA Modules:
  0.0 72.8 jit_solution(2708200856962943625)
XLA Ops:
  0.6 0.7 %copy.13.counts = s32[3,1,1]{2,1,0:T(1,128)S(1)} copy(s32[3,1,1]{0,2,1:T(1,128)} %param.13) | data formatting | bytes 24 | tf_op args[6]
  1.4 0.8 %copy.12.index = s32[3,6,2]{2,1,0:T(8,128)S(1)} copy(s32[3,6,2]{1,2,0:T(2,128)} %param.12) | data formatting | bytes 288 | tf_op args[5]
  2.2 0.0 copy-start
  2.2 0.9 %copy-done = bf16[6,128,128]{2,1,0:T(8,128)(2,1)S(1)} copy-done((bf16[6,128,128]{2,1,0:T(8,128)(2,1)S(1)}, bf16[6,128,128]{2,1,0:T(8,128)(2,1)}, u32[]{:S(2)}) %copy-start) | copy-done | bytes 196632
  3.1 0.0 copy-start.1
  3.1 0.9 %copy-done.1 = bf16[6,128,128]{2,1,0:T(8,128)(2,1)S(1)} copy-done((bf16[6,128,128]{2,1,0:T(8,128)(2,1)S(1)}, bf16[6,128,128]{2,1,0:T(8,128)(2,1)}, u32[]{:S(2)}) %copy-start.1) | copy-done | bytes 196632
  4.0 0.0 copy-start.2
  4.0 0.9 %copy-done.2 = bf16[6,128,128]{2,1,0:T(8,128)(2,1)S(1)} copy-done((bf16[6,128,128]{2,1,0:T(8,128)(2,1)S(1)}, bf16[6,128,128]{2,1,0:T(8,128)(2,1)}, u32[]{:S(2)}) %copy-start.2) | copy-done | bytes 196632
  4.9 0.0 copy-start.3
  4.9 0.9 %copy-done.3 = bf16[10,4096]{1,0:T(8,128)(2,1)S(1)} copy-done((bf16[10,4096]{1,0:T(8,128)(2,1)S(1)}, bf16[10,4096]{1,0:T(8,128)(2,1)}, u32[]{:S(2)}) %copy-start.3) | copy-done | bytes 81944
  5.8 0.0 copy-start.4
  5.8 0.9 %copy-done.4 = bf16[10,4096]{1,0:T(8,128)(2,1)S(1)} copy-done((bf16[10,4096]{1,0:T(8,128)(2,1)S(1)}, bf16[10,4096]{1,0:T(8,128)(2,1)}, u32[]{:S(2)}) %copy-start.4) | copy-done | bytes 81944
  6.7 62.5 %exchange.1 = (bf16[16,192,128]{2,1,0:T(8,128)(2,1)S(1)}, s32[18,8,128]{2,1,0:T(8,128)S(1)}, f32[6,128,128]{2,1,0:T(8,128)S(1)}, f32[6,128,128]{2,1,0:T(8,128)S(1)}, f32[6,128,128]{2,1,0:T(8,128)S(1)}) custom-call(s32[3,6,2]{2,1,0:T(8,128)S(1)} %copy.12.index, s32[3,1,1]{2,1,0:T(1,128)S(1)} %copy.13.counts, bf16[10,4096]{1,0:T(8,128)(2,1)S(1)} %copy-done.3, ...), custom_call_target="tpu_custom_call" | custom-call | tf_op jit(solution)/shard_map/exchange/pallas_call | solution.py:380
  69.3 3.5 %add_slots.1 = (bf16[10,4096]{1,0:T(8,128)(2,1)}, bf16[10,4096]{1,0:T(8,128)(2,1)}, f32[6,128,128]{2,1,0:T(8,128)}, f32[6,128,128]{2,1,0:T(8,128)}, f32[6,128,128]{2,1,0:T(8,128)}) custom-call(s32[18,8,128]{2,1,0:T(8,128)S(1)} %get-tuple-element.10.meta, bf16[16,192,128]{2,1,0:T(8,128)(2,1)S(1)} %get-tuple-element.11.got, ...), custom_call_target="tpu_custom_call" | custom-call | tf_op jit(solution)/shard_map/add_slots/pallas_call | solution.py:414
Async XLA Ops:
  2.2 0.9 %copy-start = (bf16[6,128,128]{2,1,0:T(8,128)(2,1)S(1)}, bf16[6,128,128]{2,1,0:T(8,128)(2,1)}, u32[]{:S(2)}) copy-start(bf16[6,128,128]{2,1,0:T(8,128)(2,1)} %gate_t.1) | copy-start | bytes 589828
  3.1 0.9 %copy-start.1 = (bf16[6,128,128]{2,1,0:T(8,128)(2,1)S(1)}, bf16[6,128,128]{2,1,0:T(8,128)(2,1)}, u32[]{:S(2)}) copy-start(bf16[6,128,128]{2,1,0:T(8,128)(2,1)} %up_t.1) | copy-start | bytes 589828
  4.0 0.9 %copy-start.2 = (bf16[6,128,128]{2,1,0:T(8,128)(2,1)S(1)}, bf16[6,128,128]{2,1,0:T(8,128)(2,1)}, u32[]{:S(2)}) copy-start(bf16[6,128,128]{2,1,0:T(8,128)(2,1)} %down_t.1) | copy-start | bytes 589828
  4.9 0.9 %copy-start.3 = (bf16[10,4096]{1,0:T(8,128)(2,1)S(1)}, bf16[10,4096]{1,0:T(8,128)(2,1)}, u32[]{:S(2)}) copy-start(bf16[10,4096]{1,0:T(8,128)(2,1)} %tok.1) | copy-start | bytes 245764
  5.8 0.9 %copy-start.4 = (bf16[10,4096]{1,0:T(8,128)(2,1)S(1)}, bf16[10,4096]{1,0:T(8,128)(2,1)}, u32[]{:S(2)}) copy-start(bf16[10,4096]{1,0:T(8,128)(2,1)} %cot.1) | copy-start | bytes 245764

commit v3 on v2

--- a/solution.py
+++ b/solution.py
@@ -124,7 +124,7 @@
     index, counts, tok, cot, gate_t, up_t, down_t,
     got_out, meta_out, gate_g, up_g, down_g,
     index_v, counts_v, meta, tiles_v, grads_v,
-    meta_v, meta_s, blocks, pack, send_a, recv_a, X, P, Pb, recv_b, acts, Q, send_c, recv_c,
+    meta_v, meta_s, blocks, pack, send_a, recv_a, X, P, Pb, recv_b, sums, acts, Q, send_c,
     m_send, m_recv, a_send, a_recv, b_send, b_recv, c_send, c_recv, in_sem, out_sem, local_sem,
 ):
     N = C * T
@@ -158,8 +158,8 @@
     counts_copy.wait()
     meta[...] = jnp.zeros_like(meta)
     for m in range(3):
-        meta[0:S, 2 * m:2 * m + 2] = index_v[m]
-        meta[S:S + 1, m:m + 1] = counts_v[m]
+        meta[2 * m:2 * m + 2, 0:S] = index_v[m]
+    meta[6:7, 0:3] = counts_v[0]
     pl.semaphore_wait(barrier, C)
 
     def meta_copy(k, owner, target):
@@ -207,7 +207,7 @@
         for s in range(3 * S):
             m = s // S
             side, base = (1, RB) if m == 2 else (0, 0)
-            b = meta_s[dest, s % S, 2 * m + side] + base
+            b = meta_s[dest, 2 * m + side, s % S] + base
             pack[s * T:(s + 1) * T, :] = blocks[b, 0:T, :]
 
     def a_start(k, _):
@@ -231,7 +231,7 @@
         return 0
 
     def live(m, s):
-        return s < meta_s[mc, S, m]
+        return s < meta_s[mc, 6, m]
 
     def b_copy(g, m):
         return pltpu.make_async_remote_copy(
@@ -240,95 +240,104 @@
             device_id={"row": partner}, device_id_type=MESH,
         )
 
-    for g in range(G):
+    def c_copy(k, owner, target):
+        return pltpu.make_async_remote_copy(
+            src_ref=send_c.at[k], dst_ref=got_out.at[owner], send_sem=c_send.at[k], recv_sem=c_recv.at[k],
+            device_id={"col": target}, device_id_type=MESH,
+        )
+
+    def c_start(k, _):
+        for s in range(3 * S):
+            pack[s * T:(s + 1) * T, :] = Q[s, pl.ds(k * T, T), :]
+        send_c[k] = pack[...].astype(BF16)
+        c_copy(k, mc, lax.rem(mc - k + C, C)).start()
+        return 0
+
+    def forward(g):
         rows = slice(g * H, (g + 1) * H)
         lax.fori_loop(max(1, g * peers), (g + 1) * peers, a_wait, 0)
         if g == 0:
             for copy in tile_copies:
                 copy.wait()
         for m in range(3):
-            def product(s, _, m=m, g=g, rows=rows):
+            for s in range(S):
                 part = dot(X[m * S + s, rows, :].astype(BF16), tiles_v[m, s], NT if m == 2 else NN)
                 part = jnp.where(live(m, s), part, 0.0)
                 P[m * S + s, rows, :] = part
-                Pb[g, m, s] = part.astype(BF16)
-                return 0
-
-            lax.fori_loop(0, S, product, 0)
+                Pb[g, m, s, 0:H, :] = part.astype(BF16)
             b_copy(g, m).start()
 
-    def c_copy(k, owner, target):
-        return pltpu.make_async_remote_copy(
-            src_ref=send_c.at[k], dst_ref=recv_c.at[owner], send_sem=c_send.at[k], recv_sem=c_recv.at[k],
-            device_id={"col": target}, device_id_type=MESH,
-        )
-
-    def c_start(k, _):
-        for s in range(3 * S):
-            pack[s * T:(s + 1) * T, :] = Q[s, pl.ds(k * T, T), :]
-        send_c[k] = pack[...].astype(BF16)
-        c_copy(k, mc, lax.rem(mc - k + C, C)).start()
-        return 0
-
-    for g in range(G):
-        rows = slice(g * H, (g + 1) * H)
-        for m in range(3):
-            b_copy(g, m).wait()
-
-        def activate(j, _, g=g, rows=rows):
-            sums = []
+        def place(j, _):
             for m in range(3):
                 side = 0 if m == 2 else 1
                 total = jnp.zeros((H, tile), F32)
                 for s in range(S):
-                    mine = meta_s[mc, s, 2 * m + side] == j
-                    theirs = meta_s[C + partner, s, 2 * m + side] == j
+                    mine = meta_s[mc, 2 * m + side, s] == j
                     total = total + jnp.where(mine, P[m * S + s, rows, :], 0.0)
-                    total = total + jnp.where(theirs, recv_b[g, m, s].astype(F32), 0.0)
-                sums.append(total)
-            gate, up, hg = sums
+                sums[m, j, rows, :] = total
+            return 0
+
+        lax.fori_loop(0, CB, place, 0)
+
+    def backward(g):
+        rows = slice(g * H, (g + 1) * H)
+        for m in range(3):
+            b_copy(g, m).wait()
+
+        def activate(j, _):
+            whole = []
+            for m in range(3):
+                side = 0 if m == 2 else 1
+                total = sums[m, j, rows, :]
+                for s in range(S):
+                    theirs = meta_s[C + partner, 2 * m + side, s] == j
+                    total = total + jnp.where(theirs, recv_b[g, m, s, 0:H, :].astype(F32), 0.0)
+                whole.append(total)
+            gate, up, hg = whole
             sg = jax.nn.sigmoid(gate)
             active = gate * sg
-            acts[0, j, rows, :] = (hg * up * sg * (1.0 + gate * (1.0 - sg))).astype(BF16)
-            acts[1, j, rows, :] = (hg * active).astype(BF16)
-            acts[2, j, rows, :] = (active * up).astype(BF16)
+            acts[0, j, rows, :] = hg * up * sg * (1.0 + gate * (1.0 - sg))
+            acts[1, j, rows, :] = hg * active
+            acts[2, j, rows, :] = active * up
             return 0
 
         lax.fori_loop(0, CB, activate, 0)
-
         for m in range(3):
-            def back(s, _, m=m, rows=rows):
-                j = meta_s[mc, s, 2 * m + (0 if m == 2 else 1)]
-                part = dot(acts[m, j, rows, :], tiles_v[m, s], NN if m == 2 else NT)
+            for s in range(S):
+                j = meta_s[mc, 2 * m + (0 if m == 2 else 1), s]
+                part = dot(acts[m, j, rows, :].astype(BF16), tiles_v[m, s], NN if m == 2 else NT)
                 Q[m * S + s, rows, :] = jnp.where(live(m, s), part, 0.0)
-                return 0
-
-            lax.fori_loop(0, S, back, 0)
         lax.fori_loop(max(1, g * peers), (g + 1) * peers, c_start, 0)
+
+    for g in range(G):
+        forward(g)
+        if g >= 1:
+            backward(g - 1)
+    backward(G - 1)
 
     for s in range(3 * S):
         pack[s * T:(s + 1) * T, :] = Q[s, 0:T, :]
-    got_out[mc] = pack[...].astype(BF16)
+    send_c[0] = pack[...].astype(BF16)
+    own_copy = pltpu.make_async_copy(send_c.at[0], got_out.at[mc], local_sem)
+    own_copy.start()
     meta_out[...] = meta_v[...]
 
     for m in range(3):
-        def tile_grad(s, _, m=m):
-            j = meta_s[mc, s, 2 * m + (0 if m == 2 else 1)]
+        for s in range(S):
+            j = meta_s[mc, 2 * m + (0 if m == 2 else 1), s]
             x = X[m * S + s].astype(BF16)
-            part = dot(acts[m, j], x, TN) if m == 2 else dot(x, acts[m, j], TN)
+            act = acts[m, j].astype(BF16)
+            part = dot(act, x, TN) if m == 2 else dot(x, act, TN)
             grads_v[m, s] = jnp.where(live(m, s), part, 0.0)
-            return 0
-
-        lax.fori_loop(0, S, tile_grad, 0)
         grad_copies[m].start()
 
     def c_wait(k, _):
         src = lax.rem(mc + k, C)
         c_copy(k, src, lax.rem(mc - k + C, C)).wait()
-        got_out[src] = recv_c[src]
         return 0
 
     lax.fori_loop(1, C, c_wait, 0)
+    own_copy.wait()
     for copy in grad_copies:
         copy.wait()
 
@@ -350,7 +359,7 @@
         for s in range(3 * S):
             m = s // S
             side, base = (1, RB) if m == 2 else (0, 0)
-            b = meta[c, s % S, 2 * m + side] + base
+            b = meta[c, 2 * m + side, s % S] + base
             total[b, 0:T, :] += pack[s * T:(s + 1) * T, :]
         return 0
 
@@ -370,22 +379,23 @@
     N = C * T
     rows = -(-3 * S * T // 16) * 16
     pad_t = -(-T // 8) * 8
-    G = 2 if C % 2 == 0 and (N // 2) % 16 == 0 else 1
-    H = N // G
-    meta_rows = -(-(S + 1) // 8) * 8
+    G = max(g for g in (1, 2, 4) if C % g == 0 and C // g * T % 8 == 0)
+    padded = -(-(N // G) // 16) * 16
+    meta_rows = 8
+    index, counts = tile_index.transpose(0, 2, 1), tile_counts.transpose(1, 2, 0)
     V, M = pltpu.VMEM, pltpu.SemaphoreType.DMA
     vspec = pl.BlockSpec(memory_space=pltpu.VMEM)
-    hbm = pl.BlockSpec(memory_space=pl.ANY)
+    hbm = pl.BlockSpec(memory_space=pltpu.HBM)
     sd = jax.ShapeDtypeStruct
     got, metas, gate_grad, up_grad, down_grad = pl.pallas_call(
         functools.partial(exchange_kernel, C, S, T, RB, CB, tile, G),
         out_shape=[sd((C, rows, tile), BF16), sd((C + R, meta_rows, 128), jnp.int32)]
         + [sd((S, tile, tile), F32)] * 3,
         in_specs=[hbm] * 2 + [vspec] * 2 + [hbm] * 3,
-        out_specs=[vspec] * 2 + [hbm] * 3,
+        out_specs=[hbm, vspec] + [hbm] * 3,
         scratch_shapes=[
-            V(tile_index.shape, jnp.int32),
-            V(tile_counts.shape, jnp.int32),
+            V(index.shape, jnp.int32),
+            V(counts.shape, jnp.int32),
             V((meta_rows, 128), jnp.int32),
             V((3, S, tile, tile), BF16),
             V((3, S, tile, tile), F32),
@@ -397,27 +407,27 @@
             V((C, rows, tile), BF16),
             V((3 * S, N, tile), F32),
             V((3 * S, N, tile), F32),
-            V((G, 3, S, H, tile), BF16),
-            V((G, 3, S, H, tile), BF16),
-            V((3, CB, N, tile), BF16),
+            V((G, 3, S, padded, tile), BF16),
+            V((G, 3, S, padded, tile), BF16),
+            V((3, CB, N, tile), F32),
+            V((3, CB, N, tile), F32),
             V((3 * S, N, tile), F32),
-            V((C, rows, tile), BF16),
             V((C, rows, tile), BF16),
             M((C,)), M((C,)), M((C,)), M((C,)), M((G, 3)), M((G, 3)), M((C,)), M((C,)),
             M((5,)), M((3,)), M,
         ],
         compiler_params=pltpu.CompilerParams(
-            collective_id=0, has_side_effects=True, vmem_limit_bytes=40 * 1024 * 1024
+            collective_id=0, has_side_effects=True, vmem_limit_bytes=60 * 1024 * 1024
         ),
         name="exchange",
-    )(tile_index, tile_counts, tokens, cotangent, gate_tiles, up_tiles, down_tiles)
+    )(index, counts, tokens, cotangent, gate_tiles, up_tiles, down_tiles)
     return pl.pallas_call(
         functools.partial(add_kernel, C, S, T, RB, tile),
         out_shape=[sd((T, width), BF16)] * 2 + [sd((S, tile, tile), F32)] * 3,
         in_specs=[pl.BlockSpec(memory_space=pltpu.SMEM), vspec] + [hbm] * 3,
         out_specs=[vspec] * 2 + [hbm] * 3,
         scratch_shapes=[V((2 * RB, pad_t, tile), F32), V((rows, tile), F32), M((3,))],
-        compiler_params=pltpu.CompilerParams(vmem_limit_bytes=16 * 1024 * 1024),
+        compiler_params=pltpu.CompilerParams(vmem_limit_bytes=60 * 1024 * 1024),
         name="add_slots",
     )(metas, got, gate_grad, up_grad, down_grad)
 

time: 73 us -> 95.4 us (1.31)
  Pallas kernels: 66 us -> 94.5 us
  local copies, waits for them, and re-layouts: 6.11 us -> 0 us
    pallas_call x1, Pallas kernels: 3.47 us -> 39.4 us  [sparse_body(): pl.pallas_call(functools.partial(add_kernel, C, S, T, RB, tile), out_shap...]
    pallas_call x1, Pallas kernels: 62.5 us -> 55.1 us  [sparse_body(): pl.pallas_call(functools.partial(exchange_kernel, C, S, T, RB, CB, tile,...]
    unnamed x12 -> x0, local copies, waits for them, and re-layouts: 6.11 us -> none
where the time goes in v3:
time: 95.4 us; the launch traced here: 95.2 us
  Pallas kernels  94.5 us (99%)
    pallas_call x1, Pallas kernels, sparse_body(): pl.pallas_call(functools.partial(exchange_kernel, C, S, T, RB, CB, tile,...  55.1 us
    pallas_call x1, Pallas kernels, sparse_body(): pl.pallas_call(functools.partial(add_kernel, C, S, T, RB, tile), out_shap...  39.4 us

profile of v3, /device:TPU:0, one launch (start us, length us, event | category | flops | bytes accessed | tf_op | source)
XLA Modules:
  0.0 95.2 jit_solution(17231492523001381314)
XLA Ops:
  0.6 55.1 %exchange.1 = (bf16[16,192,128]{2,1,0:T(8,128)(2,1)}, s32[18,8,128]{2,1,0:T(8,128)}, f32[6,128,128]{2,1,0:T(8,128)}, f32[6,128,128]{2,1,0:T(8,128)}, f32[6,128,128]{2,1,0:T(8,128)}) custom-call(s32[3,2,6]{2,1,0:T(2,128)} %bitcast.2, s32[1,1,3]{2,1,0:T(1,128)} %bitcast.3, bf16[10,4096]{1,0:T(8,128)(2,1)} %tok.1, bf16[10,4096]{1,0:T(8,128)(2,1)} %cot.1, ...), custom_call_target="tpu_custom_call" | custom-call | tf_op jit(solution)/shard_map/exchange/pallas_call | solution.py:390
  55.7 39.4 %add_slots.1 = (bf16[10,4096]{1,0:T(8,128)(2,1)}, bf16[10,4096]{1,0:T(8,128)(2,1)}, f32[6,128,128]{2,1,0:T(8,128)}, f32[6,128,128]{2,1,0:T(8,128)}, f32[6,128,128]{2,1,0:T(8,128)}) custom-call(s32[18,8,128]{2,1,0:T(8,128)} %get-tuple-element.10.meta, bf16[16,192,128]{2,1,0:T(8,128)(2,1)} %get-tuple-element.11.got, f32[6,128,128]{2,1,0:T(8,128)} %get-tuple-element.12.gate_in, ...), custom_call_target="tpu_custom_call" | custom-call | tf_op jit(solution)/shard_map/add_slots/pallas_call | solution.py:424

commit v4 on v3

--- a/solution.py
+++ b/solution.py
@@ -344,13 +344,17 @@
 
 def add_kernel(
     C, S, T, RB, tile, meta, got, gate_in, up_in, down_in,
-    out, ingrad, gate_g, up_g, down_g, total, pack, sem,
+    out, ingrad, gate_g, up_g, down_g, total, pack, held, load_sem, store_sem,
 ):
-    copies = [
-        pltpu.make_async_copy(src, dst, sem.at[m])
-        for m, (src, dst) in enumerate(((gate_in, gate_g), (up_in, up_g), (down_in, down_g)))
+    loads = [
+        pltpu.make_async_copy(src, held.at[m], load_sem.at[m])
+        for m, src in enumerate((gate_in, up_in, down_in))
     ]
-    for copy in copies:
+    stores = [
+        pltpu.make_async_copy(held.at[m], dst, store_sem.at[m])
+        for m, dst in enumerate((gate_g, up_g, down_g))
+    ]
+    for copy in loads:
         copy.start()
     total[...] = jnp.zeros_like(total)
 
@@ -364,11 +368,14 @@
         return 0
 
     lax.fori_loop(0, C, add, 0)
+    for load, store in zip(loads, stores):
+        load.wait()
+        store.start()
     for b in range(RB):
         ingrad[:, b * tile:(b + 1) * tile] = total[b, 0:T, :].astype(BF16)
         out[:, b * tile:(b + 1) * tile] = total[RB + b, 0:T, :].astype(BF16)
-    for copy in copies:
-        copy.wait()
+    for store in stores:
+        store.wait()
 
 
 def sparse_body(tokens, cotangent, gate_tiles, up_tiles, down_tiles, tile_index, tile_counts):
@@ -426,7 +433,10 @@
         out_shape=[sd((T, width), BF16)] * 2 + [sd((S, tile, tile), F32)] * 3,
         in_specs=[pl.BlockSpec(memory_space=pltpu.SMEM), vspec] + [hbm] * 3,
         out_specs=[vspec] * 2 + [hbm] * 3,
-        scratch_shapes=[V((2 * RB, pad_t, tile), F32), V((rows, tile), F32), M((3,))],
+        scratch_shapes=[
+            V((2 * RB, pad_t, tile), F32), V((rows, tile), F32),
+            V((3, S, tile, tile), F32), M((3,)), M((3,)),
+        ],
         compiler_params=pltpu.CompilerParams(vmem_limit_bytes=60 * 1024 * 1024),
         name="add_slots",
     )(metas, got, gate_grad, up_grad, down_grad)

time: 95.4 us -> 60.7 us (0.64)
  Pallas kernels: 94.5 us -> 59.8 us
    pallas_call x1, Pallas kernels: 39.4 us -> 4.7 us  [sparse_body(): pl.pallas_call(functools.partial(add_kernel, C, S, T, RB, tile), out_shap...]
where the time goes in v4:
time: 60.7 us; the launch traced here: 60.5 us
  Pallas kernels  59.8 us (99%)
  between operations  0.64 us (1%)
    pallas_call x1, Pallas kernels, sparse_body(): pl.pallas_call(functools.partial(exchange_kernel, C, S, T, RB, CB, tile,...  55.1 us
    pallas_call x1, Pallas kernels, sparse_body(): pl.pallas_call(functools.partial(add_kernel, C, S, T, RB, tile), out_shap...  4.7 us

profile of v4, /device:TPU:0, one launch (start us, length us, event | category | flops | bytes accessed | tf_op | source)
XLA Modules:
  0.0 60.5 jit_solution(1018204040516467837)
XLA Ops:
  0.6 55.1 %exchange.1 = (bf16[16,192,128]{2,1,0:T(8,128)(2,1)}, s32[18,8,128]{2,1,0:T(8,128)}, f32[6,128,128]{2,1,0:T(8,128)}, f32[6,128,128]{2,1,0:T(8,128)}, f32[6,128,128]{2,1,0:T(8,128)}) custom-call(s32[3,2,6]{2,1,0:T(2,128)} %bitcast.2, s32[1,1,3]{2,1,0:T(1,128)} %bitcast.3, bf16[10,4096]{1,0:T(8,128)(2,1)} %tok.1, bf16[10,4096]{1,0:T(8,128)(2,1)} %cot.1, ...), custom_call_target="tpu_custom_call" | custom-call | tf_op jit(solution)/shard_map/exchange/pallas_call | solution.py:397
  55.7 4.7 %add_slots.1 = (bf16[10,4096]{1,0:T(8,128)(2,1)}, bf16[10,4096]{1,0:T(8,128)(2,1)}, f32[6,128,128]{2,1,0:T(8,128)}, f32[6,128,128]{2,1,0:T(8,128)}, f32[6,128,128]{2,1,0:T(8,128)}) custom-call(s32[18,8,128]{2,1,0:T(8,128)} %get-tuple-element.10.meta, bf16[16,192,128]{2,1,0:T(8,128)(2,1)} %get-tuple-element.11.got, f32[6,128,128]{2,1,0:T(8,128)} %get-tuple-element.12.gate_in, ...), custom_call_target="tpu_custom_call" | custom-call | tf_op jit(solution)/shard_map/add_slots/pallas_call | solution.py:431

commit v5 on v4

--- a/solution.py
+++ b/solution.py
@@ -108,6 +108,7 @@
 
 
 MESH = pl.DeviceIdType.MESH
+PLANE = 4
 F32 = jnp.float32
 BF16 = jnp.bfloat16
 NT = (((1,), (1,)), ((), ()))
@@ -123,12 +124,13 @@
     C, S, T, RB, CB, tile, G,
     index, counts, tok, cot, gate_t, up_t, down_t,
     got_out, meta_out, gate_g, up_g, down_g,
-    index_v, counts_v, meta, tiles_v, grads_v,
+    index_v, counts_v, meta, tiles_v, grads_v, flat, dense,
     meta_v, meta_s, blocks, pack, send_a, recv_a, X, P, Pb, recv_b, sums, acts, Q, send_c,
-    m_send, m_recv, a_send, a_recv, b_send, b_recv, c_send, c_recv, in_sem, out_sem, local_sem,
+    m_send, m_recv, a_send, a_recv, b_send, b_recv, c_send, c_recv, l_send, l_recv, in_sem, out_sem,
+    local_sem, save_sem,
 ):
     N = C * T
-    H, peers = N // G, C // G
+    H = N // G
     mc, mr = lax.axis_index("col"), lax.axis_index("row")
     partner = 1 - mr
     index_copy = pltpu.make_async_copy(index, index_v, in_sem.at[3])
@@ -160,12 +162,30 @@
     for m in range(3):
         meta[2 * m:2 * m + 2, 0:S] = index_v[m]
     meta[6:7, 0:3] = counts_v[0]
+    for b in range(RB):
+        flat[b * T:(b + 1) * T, :] = tok[:, b * tile:(b + 1) * tile].astype(F32)
+        flat[(RB + b) * T:(RB + b + 1) * T, :] = cot[:, b * tile:(b + 1) * tile].astype(F32)
     pl.semaphore_wait(barrier, C)
 
-    def meta_copy(k, owner, target):
+    line, here = C // PLANE, lax.rem(mc, PLANE)
+    z = lax.div(mc, PLANE)
+
+    def ahead(k):
+        return lax.rem(mc + k, C)
+
+    def behind(k):
+        return lax.rem(mc - k + C, C)
+
+    def peer(q):
+        return z * PLANE + lax.rem(here + q, PLANE)
+
+    def source(q):
+        return lax.rem(here - q + PLANE, PLANE)
+
+    def meta_copy(k, owner):
         return pltpu.make_async_remote_copy(
             src_ref=meta, dst_ref=meta_v.at[owner], send_sem=m_send.at[k], recv_sem=m_recv.at[k],
-            device_id={"col": target}, device_id_type=MESH,
+            device_id={"col": ahead(k)}, device_id_type=MESH,
         )
 
     def meta_row(owner):
@@ -174,33 +194,49 @@
             device_id={"row": partner}, device_id_type=MESH,
         )
 
-    def meta_start(k, _):
-        meta_copy(k, mc, lax.rem(mc + k, C)).start()
-        return 0
-
-    lax.fori_loop(1, C, meta_start, 0)
+    def line_copy(origin, up):
+        return pltpu.make_async_remote_copy(
+            src_ref=dense.at[origin], dst_ref=dense.at[origin],
+            send_sem=l_send.at[origin, up], recv_sem=l_recv.at[origin],
+            device_id={"col": mc + PLANE if up else mc - PLANE}, device_id_type=MESH,
+        )
+
+    for k in range(1, PLANE):
+        meta_copy(k, mc).start()
+    dense[z] = flat[...].astype(BF16)
+
+    @pl.when(z < line - 1)
+    def _():
+        line_copy(z, 1).start()
+
+    @pl.when(z > 0)
+    def _():
+        line_copy(z, 0).start()
+
+    for k in range(PLANE, C):
+        meta_copy(k, mc).start()
     meta_row(mr).start()
     meta_v[mc] = meta[...]
     meta_v[C + mr] = meta[...]
-    for b in range(RB):
-        blocks[b, 0:T, :] = tok[:, b * tile:(b + 1) * tile].astype(F32)
-        blocks[RB + b, 0:T, :] = cot[:, b * tile:(b + 1) * tile].astype(F32)
     pack[...] = jnp.zeros_like(pack)
-
-    def meta_wait(k, _):
-        meta_copy(k, lax.rem(mc - k + C, C), lax.rem(mc + k, C)).wait()
-        return 0
-
-    lax.fori_loop(1, C, meta_wait, 0)
+    for k in range(1, C):
+        meta_copy(k, behind(k)).wait()
     meta_row(partner).wait()
     to_smem = pltpu.make_async_copy(meta_v, meta_s, local_sem)
     to_smem.start()
     to_smem.wait()
-
-    def a_copy(k, owner, target):
+    meta_save = pltpu.make_async_copy(meta_v, meta_out, save_sem)
+    meta_save.start()
+
+    def origin_of(t):
+        half = lax.div(z, 2)
+        return (z, z + 1 - 2 * lax.rem(z, 2), 2 - half, 3 - 3 * half)[t]
+
+    def a_copy(t, q, owner):
         return pltpu.make_async_remote_copy(
-            src_ref=send_a.at[k], dst_ref=recv_a.at[owner], send_sem=a_send.at[k], recv_sem=a_recv.at[k],
-            device_id={"col": target}, device_id_type=MESH,
+            src_ref=send_a.at[t, q], dst_ref=recv_a.at[t, owner],
+            send_sem=a_send.at[t, q], recv_sem=a_recv.at[t, q],
+            device_id={"col": peer(q)}, device_id_type=MESH,
         )
 
     def pick_for(dest):
@@ -210,25 +246,41 @@
             b = meta_s[dest, 2 * m + side, s % S] + base
             pack[s * T:(s + 1) * T, :] = blocks[b, 0:T, :]
 
-    def a_start(k, _):
-        dest = lax.rem(mc + k, C)
-        pick_for(dest)
-        send_a[k] = pack[...].astype(BF16)
-        a_copy(k, mc, dest).start()
-        return 0
-
-    lax.fori_loop(1, C, a_start, 0)
-    pick_for(mc)
-    for s in range(3 * S):
-        X[s, 0:T, :] = pack[s * T:(s + 1) * T, :]
-
-    def a_wait(k, _):
-        src = lax.rem(mc - k + C, C)
-        a_copy(k, src, lax.rem(mc + k, C)).wait()
-        pack[...] = recv_a[src].astype(F32)
+    def stage(t):
+        if t > 0:
+            origin = origin_of(t)
+            line_copy(origin, 0).wait_recv()
+
+            @pl.when((origin < z) & (z < line - 1))
+            def _():
+                line_copy(origin, 1).start()
+
+            @pl.when((origin > z) & (z > 0))
+            def _():
+                line_copy(origin, 0).start()
+
+            flat[...] = dense[origin].astype(F32)
+        for b in range(2 * RB):
+            blocks[b, 0:T, :] = flat[b * T:(b + 1) * T, :]
+
+        def send(q, _):
+            pick_for(peer(q))
+            send_a[t, q] = pack[...].astype(BF16)
+            a_copy(t, q, here).start()
+            return 0
+
+        lax.fori_loop(1, PLANE, send, 0)
+        pick_for(mc)
         for s in range(3 * S):
-            X[s, pl.ds(k * T, T), :] = pack[s * T:(s + 1) * T, :]
-        return 0
+            X[s, t * PLANE * T:t * PLANE * T + T, :] = pack[s * T:(s + 1) * T, :]
+
+    def a_wait(t):
+        for q in range(1, PLANE):
+            a_copy(t, q, source(q)).wait()
+            pack[...] = recv_a[t, source(q)].astype(F32)
+            at = (t * PLANE + q) * T
+            for s in range(3 * S):
+                X[s, at:at + T, :] = pack[s * T:(s + 1) * T, :]
 
     def live(m, s):
         return s < meta_s[mc, 6, m]
@@ -240,22 +292,33 @@
             device_id={"row": partner}, device_id_type=MESH,
         )
 
-    def c_copy(k, owner, target):
+    def c_copy(k, dest, owner, turn):
         return pltpu.make_async_remote_copy(
-            src_ref=send_c.at[k], dst_ref=got_out.at[owner], send_sem=c_send.at[k], recv_sem=c_recv.at[k],
-            device_id={"col": target}, device_id_type=MESH,
+            src_ref=send_c.at[k], dst_ref=got_out.at[owner],
+            send_sem=c_send.at[k], recv_sem=c_recv.at[turn],
+            device_id={"col": dest}, device_id_type=MESH,
         )
 
-    def c_start(k, _):
+    def c_pack(k):
         for s in range(3 * S):
-            pack[s * T:(s + 1) * T, :] = Q[s, pl.ds(k * T, T), :]
+            pack[s * T:(s + 1) * T, :] = Q[s, k * T:(k + 1) * T, :]
         send_c[k] = pack[...].astype(BF16)
-        c_copy(k, mc, lax.rem(mc - k + C, C)).start()
-        return 0
+
+    def c_dest(k):
+        return origin_of(k // PLANE) * PLANE + source(k % PLANE)
+
+    own_copy = pltpu.make_async_copy(send_c.at[0], got_out.at[mc], local_sem)
+
+    def c_start(k):
+        c_pack(k)
+        if k == 0:
+            own_copy.start()
+        else:
+            c_copy(k, c_dest(k), mc, lax.rem(mc - c_dest(k) + C, C)).start()
 
     def forward(g):
         rows = slice(g * H, (g + 1) * H)
-        lax.fori_loop(max(1, g * peers), (g + 1) * peers, a_wait, 0)
+        a_wait(g)
         if g == 0:
             for copy in tile_copies:
                 copy.wait()
@@ -307,20 +370,17 @@
                 j = meta_s[mc, 2 * m + (0 if m == 2 else 1), s]
                 part = dot(acts[m, j, rows, :].astype(BF16), tiles_v[m, s], NN if m == 2 else NT)
                 Q[m * S + s, rows, :] = jnp.where(live(m, s), part, 0.0)
-        lax.fori_loop(max(1, g * peers), (g + 1) * peers, c_start, 0)
-
+        for k in range(g * PLANE, (g + 1) * PLANE):
+            c_start(k)
+
+    stage(0)
     for g in range(G):
+        if g + 1 < G:
+            stage(g + 1)
         forward(g)
         if g >= 1:
             backward(g - 1)
     backward(G - 1)
-
-    for s in range(3 * S):
-        pack[s * T:(s + 1) * T, :] = Q[s, 0:T, :]
-    send_c[0] = pack[...].astype(BF16)
-    own_copy = pltpu.make_async_copy(send_c.at[0], got_out.at[mc], local_sem)
-    own_copy.start()
-    meta_out[...] = meta_v[...]
 
     for m in range(3):
         for s in range(S):
@@ -331,12 +391,21 @@
             grads_v[m, s] = jnp.where(live(m, s), part, 0.0)
         grad_copies[m].start()
 
-    def c_wait(k, _):
-        src = lax.rem(mc + k, C)
-        c_copy(k, src, lax.rem(mc - k + C, C)).wait()
-        return 0
-
-    lax.fori_loop(1, C, c_wait, 0)
+    for k in range(1, C):
+        dest = c_dest(k)
+        c_copy(k, dest, dest, lax.rem(dest - mc + C, C)).wait()
+    for t in range(line):
+        origin = origin_of(t)
+
+        @pl.when((origin <= z) & (z < line - 1))
+        def _():
+            line_copy(origin, 1).wait_send()
+
+        @pl.when((origin >= z) & (z > 0))
+        def _():
+            line_copy(origin, 0).wait_send()
+
+    meta_save.wait()
     own_copy.wait()
     for copy in grad_copies:
         copy.wait()
@@ -386,7 +455,7 @@
     N = C * T
     rows = -(-3 * S * T // 16) * 16
     pad_t = -(-T // 8) * 8
-    G = max(g for g in (1, 2, 4) if C % g == 0 and C // g * T % 8 == 0)
+    G = C // PLANE
     padded = -(-(N // G) // 16) * 16
     meta_rows = 8
     index, counts = tile_index.transpose(0, 2, 1), tile_counts.transpose(1, 2, 0)
@@ -399,19 +468,21 @@
         out_shape=[sd((C, rows, tile), BF16), sd((C + R, meta_rows, 128), jnp.int32)]
         + [sd((S, tile, tile), F32)] * 3,
         in_specs=[hbm] * 2 + [vspec] * 2 + [hbm] * 3,
-        out_specs=[hbm, vspec] + [hbm] * 3,
+        out_specs=[hbm] * 5,
         scratch_shapes=[
             V(index.shape, jnp.int32),
             V(counts.shape, jnp.int32),
             V((meta_rows, 128), jnp.int32),
             V((3, S, tile, tile), BF16),
             V((3, S, tile, tile), F32),
+            V((2 * RB * T, tile), F32),
+            V((G, 2 * RB * T, tile), BF16),
             V((C + R, meta_rows, 128), jnp.int32),
             pltpu.SMEM((C + R, meta_rows, 128), jnp.int32),
             V((2 * RB, pad_t, tile), F32),
             V((rows, tile), F32),
-            V((C, rows, tile), BF16),
-            V((C, rows, tile), BF16),
+            V((G, PLANE, rows, tile), BF16),
+            V((G, PLANE, rows, tile), BF16),
             V((3 * S, N, tile), F32),
             V((3 * S, N, tile), F32),
             V((G, 3, S, padded, tile), BF16),
@@ -420,8 +491,8 @@
             V((3, CB, N, tile), F32),
             V((3 * S, N, tile), F32),
             V((C, rows, tile), BF16),
-            M((C,)), M((C,)), M((C,)), M((C,)), M((G, 3)), M((G, 3)), M((C,)), M((C,)),
-            M((5,)), M((3,)), M,
+            M((C,)), M((C,)), M((G, PLANE)), M((G, PLANE)), M((G, 3)), M((G, 3)), M((C,)), M((C,)),
+            M((G, 2)), M((G,)), M((5,)), M((3,)), M, M,
         ],
         compiler_params=pltpu.CompilerParams(
             collective_id=0, has_side_effects=True, vmem_limit_bytes=60 * 1024 * 1024
@@ -443,7 +514,7 @@
 
 
 def solution(mesh):
-    body = sparse_body if mesh.shape["row"] == 2 else dense_body
+    body = sparse_body if (mesh.shape["row"], mesh.shape["col"]) == (2, 4 * PLANE) else dense_body
     return jax.shard_map(
         body,
         mesh=mesh,

time: 60.7 us -> 64.3 us (1.059)
  Pallas kernels: 59.8 us -> 63.5 us
    pallas_call x1, Pallas kernels: 55.1 us -> 58.8 us  [sparse_body(): pl.pallas_call(functools.partial(exchange_kernel, C, S, T, RB, CB, tile,...]
where the time goes in v5:
time: 64.3 us; the launch traced here: 64.1 us
  Pallas kernels  63.5 us (99%)
    pallas_call x1, Pallas kernels, sparse_body(): pl.pallas_call(functools.partial(exchange_kernel, C, S, T, RB, CB, tile,...  58.8 us
    pallas_call x1, Pallas kernels, sparse_body(): pl.pallas_call(functools.partial(add_kernel, C, S, T, RB, tile), out_shap...  4.7 us

profile of v5, /device:TPU:0, one launch (start us, length us, event | category | flops | bytes accessed | tf_op | source)
XLA Modules:
  0.0 64.1 jit_solution(14617051977761139018)
XLA Ops:
  0.6 58.8 %exchange.1 = (bf16[16,192,128]{2,1,0:T(8,128)(2,1)}, s32[18,8,128]{2,1,0:T(8,128)}, f32[6,128,128]{2,1,0:T(8,128)}, f32[6,128,128]{2,1,0:T(8,128)}, f32[6,128,128]{2,1,0:T(8,128)}) custom-call(s32[3,2,6]{2,1,0:T(2,128)} %bitcast.2, s32[1,1,3]{2,1,0:T(1,128)} %bitcast.3, bf16[10,4096]{1,0:T(8,128)(2,1)} %tok.1, bf16[10,4096]{1,0:T(8,128)(2,1)} %cot.1, ...), custom_call_target="tpu_custom_call" | custom-call | tf_op jit(solution)/shard_map/exchange/pallas_call | solution.py:466
  59.4 4.7 %add_slots.1 = (bf16[10,4096]{1,0:T(8,128)(2,1)}, bf16[10,4096]{1,0:T(8,128)(2,1)}, f32[6,128,128]{2,1,0:T(8,128)}, f32[6,128,128]{2,1,0:T(8,128)}, f32[6,128,128]{2,1,0:T(8,128)}) custom-call(s32[18,8,128]{2,1,0:T(8,128)} %get-tuple-element.10.meta, bf16[16,192,128]{2,1,0:T(8,128)(2,1)} %get-tuple-element.11.got, f32[6,128,128]{2,1,0:T(8,128)} %get-tuple-element.12.gate_in, ...), custom_call_target="tpu_custom_call" | custom-call | tf_op jit(solution)/shard_map/add_slots/pallas_call | solution.py:502

commit v6 on v4

--- a/solution.py
+++ b/solution.py
@@ -126,6 +126,7 @@
     index_v, counts_v, meta, tiles_v, grads_v,
     meta_v, meta_s, blocks, pack, send_a, recv_a, X, P, Pb, recv_b, sums, acts, Q, send_c,
     m_send, m_recv, a_send, a_recv, b_send, b_recv, c_send, c_recv, in_sem, out_sem, local_sem,
+    save_sem,
 ):
     N = C * T
     H, peers = N // G, C // G
@@ -196,6 +197,8 @@
     to_smem = pltpu.make_async_copy(meta_v, meta_s, local_sem)
     to_smem.start()
     to_smem.wait()
+    meta_save = pltpu.make_async_copy(meta_v, meta_out, save_sem)
+    meta_save.start()
 
     def a_copy(k, owner, target):
         return pltpu.make_async_remote_copy(
@@ -320,7 +323,6 @@
     send_c[0] = pack[...].astype(BF16)
     own_copy = pltpu.make_async_copy(send_c.at[0], got_out.at[mc], local_sem)
     own_copy.start()
-    meta_out[...] = meta_v[...]
 
     for m in range(3):
         for s in range(S):
@@ -338,6 +340,7 @@
 
     lax.fori_loop(1, C, c_wait, 0)
     own_copy.wait()
+    meta_save.wait()
     for copy in grad_copies:
         copy.wait()
 
@@ -386,7 +389,7 @@
     N = C * T
     rows = -(-3 * S * T // 16) * 16
     pad_t = -(-T // 8) * 8
-    G = max(g for g in (1, 2, 4) if C % g == 0 and C // g * T % 8 == 0)
+    G = max(g for g in (1, 2) if C % g == 0 and C // g * T % 8 == 0)
     padded = -(-(N // G) // 16) * 16
     meta_rows = 8
     index, counts = tile_index.transpose(0, 2, 1), tile_counts.transpose(1, 2, 0)
@@ -399,7 +402,7 @@
         out_shape=[sd((C, rows, tile), BF16), sd((C + R, meta_rows, 128), jnp.int32)]
         + [sd((S, tile, tile), F32)] * 3,
         in_specs=[hbm] * 2 + [vspec] * 2 + [hbm] * 3,
-        out_specs=[hbm, vspec] + [hbm] * 3,
+        out_specs=[hbm] * 5,
         scratch_shapes=[
             V(index.shape, jnp.int32),
             V(counts.shape, jnp.int32),
@@ -421,7 +424,7 @@
             V((3 * S, N, tile), F32),
             V((C, rows, tile), BF16),
             M((C,)), M((C,)), M((C,)), M((C,)), M((G, 3)), M((G, 3)), M((C,)), M((C,)),
-            M((5,)), M((3,)), M,
+            M((5,)), M((3,)), M, M,
         ],
         compiler_params=pltpu.CompilerParams(
             collective_id=0, has_side_effects=True, vmem_limit_bytes=60 * 1024 * 1024

time: 60.7 us -> 65 us (1.071)
  Pallas kernels: 59.8 us -> 64.2 us
    pallas_call x1, Pallas kernels: 55.1 us -> 59.5 us  [sparse_body(): pl.pallas_call(functools.partial(exchange_kernel, C, S, T, RB, CB, tile,...]
where the time goes in v6:
time: 65 us; the launch traced here: 64.8 us
  Pallas kernels  64.2 us (99%)
    pallas_call x1, Pallas kernels, sparse_body(): pl.pallas_call(functools.partial(exchange_kernel, C, S, T, RB, CB, tile,...  59.5 us
    pallas_call x1, Pallas kernels, sparse_body(): pl.pallas_call(functools.partial(add_kernel, C, S, T, RB, tile), out_shap...  4.69 us

profile of v6, /device:TPU:0, one launch (start us, length us, event | category | flops | bytes accessed | tf_op | source)
XLA Modules:
  0.0 64.8 jit_solution(3251321884628445921)
XLA Ops:
  0.6 59.5 %exchange.1 = (bf16[16,192,128]{2,1,0:T(8,128)(2,1)}, s32[18,8,128]{2,1,0:T(8,128)}, f32[6,128,128]{2,1,0:T(8,128)}, f32[6,128,128]{2,1,0:T(8,128)}, f32[6,128,128]{2,1,0:T(8,128)}) custom-call(s32[3,2,6]{2,1,0:T(2,128)} %bitcast.2, s32[1,1,3]{2,1,0:T(1,128)} %bitcast.3, bf16[10,4096]{1,0:T(8,128)(2,1)} %tok.1, bf16[10,4096]{1,0:T(8,128)(2,1)} %cot.1, ...), custom_call_target="tpu_custom_call" | custom-call | tf_op jit(solution)/shard_map/exchange/pallas_call | solution.py:400
  60.1 4.7 %add_slots.1 = (bf16[10,4096]{1,0:T(8,128)(2,1)}, bf16[10,4096]{1,0:T(8,128)(2,1)}, f32[6,128,128]{2,1,0:T(8,128)}, f32[6,128,128]{2,1,0:T(8,128)}, f32[6,128,128]{2,1,0:T(8,128)}) custom-call(s32[18,8,128]{2,1,0:T(8,128)} %get-tuple-element.10.meta, bf16[16,192,128]{2,1,0:T(8,128)(2,1)} %get-tuple-element.11.got, f32[6,128,128]{2,1,0:T(8,128)} %get-tuple-element.12.gate_in, ...), custom_call_target="tpu_custom_call" | custom-call | tf_op jit(solution)/shard_map/add_slots/pallas_call | solution.py:434

commit v7 on v6

--- a/solution.py
+++ b/solution.py
@@ -370,7 +370,7 @@
             total[b, 0:T, :] += pack[s * T:(s + 1) * T, :]
         return 0
 
-    lax.fori_loop(0, C, add, 0)
+    lax.fori_loop(0, C, add, 0, unroll=2)
     for load, store in zip(loads, stores):
         load.wait()
         store.start()
@@ -389,7 +389,7 @@
     N = C * T
     rows = -(-3 * S * T // 16) * 16
     pad_t = -(-T // 8) * 8
-    G = max(g for g in (1, 2) if C % g == 0 and C // g * T % 8 == 0)
+    G = max(g for g in (1, 2, 4) if C % g == 0 and C // g * T % 8 == 0)
     padded = -(-(N // G) // 16) * 16
     meta_rows = 8
     index, counts = tile_index.transpose(0, 2, 1), tile_counts.transpose(1, 2, 0)

time: 65 us -> 60.1 us (0.925)
  Pallas kernels: 64.2 us -> 59.2 us
    pallas_call x1, Pallas kernels: 59.5 us -> 54.5 us  [sparse_body(): pl.pallas_call(functools.partial(exchange_kernel, C, S, T, RB, CB, tile,...]
where the time goes in v7:
time: 60.1 us; the launch traced here: 59.9 us
  Pallas kernels  59.2 us (99%)
  between operations  0.64 us (1%)
    pallas_call x1, Pallas kernels, sparse_body(): pl.pallas_call(functools.partial(exchange_kernel, C, S, T, RB, CB, tile,...  54.5 us
    pallas_call x1, Pallas kernels, sparse_body(): pl.pallas_call(functools.partial(add_kernel, C, S, T, RB, tile), out_shap...  4.75 us

profile of v7, /device:TPU:0, one launch (start us, length us, event | category | flops | bytes accessed | tf_op | source)
XLA Modules:
  0.0 59.9 jit_solution(784616973831845601)
XLA Ops:
  0.6 54.5 %exchange.1 = (bf16[16,192,128]{2,1,0:T(8,128)(2,1)}, s32[18,8,128]{2,1,0:T(8,128)}, f32[6,128,128]{2,1,0:T(8,128)}, f32[6,128,128]{2,1,0:T(8,128)}, f32[6,128,128]{2,1,0:T(8,128)}) custom-call(s32[3,2,6]{2,1,0:T(2,128)} %bitcast.2, s32[1,1,3]{2,1,0:T(1,128)} %bitcast.3, bf16[10,4096]{1,0:T(8,128)(2,1)} %tok.1, bf16[10,4096]{1,0:T(8,128)(2,1)} %cot.1, ...), custom_call_target="tpu_custom_call" | custom-call | tf_op jit(solution)/shard_map/exchange/pallas_call | solution.py:400
  55.1 4.7 %add_slots.1 = (bf16[10,4096]{1,0:T(8,128)(2,1)}, bf16[10,4096]{1,0:T(8,128)(2,1)}, f32[6,128,128]{2,1,0:T(8,128)}, f32[6,128,128]{2,1,0:T(8,128)}, f32[6,128,128]{2,1,0:T(8,128)}) custom-call(s32[18,8,128]{2,1,0:T(8,128)} %get-tuple-element.10.meta, bf16[16,192,128]{2,1,0:T(8,128)(2,1)} %get-tuple-element.11.got, f32[6,128,128]{2,1,0:T(8,128)} %get-tuple-element.12.gate_in, ...), custom_call_target="tpu_custom_call" | custom-call | tf_op jit(solution)/shard_map/add_slots/pallas_call | solution.py:434
